TPU v7x, 512 devices: a whole 4x8x8 slice. The times are simulated.
512 devices in a mesh: wide: 64 (over y_hi, z, x), narrow: 8 (over y_lo, core).
Axes of the slice: x: 4, y: 8 (y_hi: 2, y_lo: 4; y = y_hi * 4 + y_lo), z: 8, core: 2. Of those that a mesh axis runs over, the one named last changes fastest.
Arguments:
- x_branch: bfloat16 [8, 4096, 5120], P('narrow', 'wide'), may hold values from -6 to 6
- w_kv: bfloat16 [5120, 1024], P(None, 'narrow'), may hold values from -0.078125 to 0.078125
- k_gain: float32 [512], replicated, may hold values from 0.1 to 1.9
- q_branch: bfloat16 [8, 4096, 2560], P('narrow', 'wide')
- prefix_kv: bfloat16 [8, 1024, 1024], P('narrow', 'wide')
- tree_parent: int32 [8, 64], P('narrow', 'wide'), may hold values from -1 to 3, as said below
Outputs:
- attended: bfloat16 [8, 4096, 2560], P('narrow', 'wide')
Inputs may be any that keep to these rules, and one draw needn't show every extreme that they name: `tree_parent`: branches 0 to 3 of every tree have parent -1; every other branch has a parent among them, and every one of them is a parent.
All inputs are finite; a program needn't handle non-finite values.
Results may differ from a plain program's by a relative error of at most 0.012.
Values may be sent and summed in bfloat16 or wider, within the bound.
No kernel may reach another device: no remote copies, remote signals or barrier semaphores. Data moves between devices by JAX's collectives and lax.ppermute only.
A program may use at most 64 MiB of HBM per device.

v0:
```python
import jax
import jax.numpy as jnp
from jax import lax
from jax.sharding import PartitionSpec as P

HEAD_SIZE = 128
TRUNKS = 4


neg_big = -1e30
block_keys = 512


def spread(value, axis, root):
    mine = lax.axis_index(axis) == root
    return lax.psum(jnp.where(mine, value, jnp.zeros_like(value)), axis)


def rotate_head_rows(key_rows, token_positions):
    half = HEAD_SIZE // 2
    index = jnp.arange(half, dtype=jnp.float32)
    inverse = jnp.exp(-jnp.log(jnp.float32(500000.0)) * 2.0 * index / HEAD_SIZE)
    angle = token_positions.astype(jnp.float32)[:, None, None] * inverse[None, None, :]
    cosine = jnp.cos(angle)
    sine = jnp.sin(angle)
    first = key_rows[..., :half]
    second = key_rows[..., half:]
    return jnp.concatenate(
        [first * cosine - second * sine, second * cosine + first * sine], axis=-1
    )


def attend(state, query4, block, extra):
    token_count = block.shape[0]
    width = block.shape[1] // 2
    heads_kv = width // HEAD_SIZE
    key_rows = block[:, :width].reshape(token_count, heads_kv, HEAD_SIZE)
    value_rows = block[:, width:].reshape(token_count, heads_kv, HEAD_SIZE)
    score = jnp.einsum(
        "rgjd,ngd->rgjn", query4, key_rows, preferred_element_type=jnp.float32
    ) * HEAD_SIZE ** (-0.5)
    if extra is not None:
        score = score + extra[:, None, None, :]
    high, total, summed = state
    new_high = jnp.maximum(high, jnp.max(score, axis=-1))
    factor = jnp.exp(high - new_high)
    expo = jnp.exp(score - new_high[..., None])
    total = total * factor + jnp.sum(expo, axis=-1)
    summed = summed * factor[..., None] + jnp.einsum(
        "rgjn,ngd->rgjd", expo.astype(jnp.bfloat16), value_rows, preferred_element_type=jnp.float32
    )
    return (new_high, total, summed)


def attend_long(state, query4, block):
    token_count = block.shape[0]
    blocks = -(-token_count // block_keys)
    pieces = block.reshape(blocks, block_keys, block.shape[1])
    starts = jnp.arange(blocks, dtype=jnp.int32) * block_keys

    def step(carry, item):
        piece, first = item
        valid = first + jnp.arange(block_keys, dtype=jnp.int32) < token_count
        extra = jnp.where(valid, 0.0, neg_big).astype(jnp.float32)[None, :]
        return (attend(carry, query4, piece, extra), None)

    state, unused = lax.scan(step, state, (pieces, starts))
    return state


def local(x_branch, w_kv, k_gain, q_branch, prefix_kv, tree_parent):
    rows = x_branch[0]
    token_count = rows.shape[0]
    kv = jnp.dot(
        rows, lax.all_gather(w_kv, "narrow", axis=1, tiled=True), preferred_element_type=jnp.float32
    )
    width = kv.shape[1] // 2
    heads_kv = width // HEAD_SIZE
    heads_q = q_branch.shape[2] // HEAD_SIZE
    query_group = heads_q // heads_kv
    key_rows = kv[:, :width]
    meansq = jnp.mean(key_rows * key_rows, axis=-1, keepdims=True)
    key_rows = key_rows * lax.rsqrt(meansq + 1e-06) * k_gain
    parent = tree_parent[0, 0]
    is_child = parent >= 0
    prefix_len = prefix_kv.shape[1] * lax.axis_size("wide")
    inside = jnp.arange(token_count, dtype=jnp.int32)
    token_positions = prefix_len + inside + token_count * is_child.astype(jnp.int32)
    key_rows = rotate_head_rows(
        key_rows.reshape(token_count, heads_kv, HEAD_SIZE), token_positions
    ).reshape(token_count, width)
    own = jnp.concatenate(
        [key_rows.astype(jnp.bfloat16), kv[:, width:].astype(jnp.bfloat16)], axis=1
    )
    above = jnp.zeros_like(own)
    for root in range(TRUNKS):
        got = spread(own, "wide", root)
        above = jnp.where(parent == root, got, above)
    query4 = q_branch[0].reshape(token_count, heads_kv, query_group, HEAD_SIZE)
    start_state = (
        jnp.full((token_count, heads_kv, query_group), neg_big, jnp.float32),
        jnp.zeros((token_count, heads_kv, query_group), jnp.float32),
        jnp.zeros((token_count, heads_kv, query_group, HEAD_SIZE), jnp.float32),
    )
    state = attend_long(
        start_state, query4, lax.all_gather(prefix_kv[0], "wide", axis=0, tiled=True)
    )
    with_parent = attend(state, query4, above, None)
    state = jax.tree.map(lambda new, old: jnp.where(is_child, new, old), with_parent, state)
    causal = jnp.where(inside[None, :] <= inside[:, None], 0.0, neg_big).astype(jnp.float32)
    high, total, summed = attend(state, query4, own, causal)
    result = (
        (summed / total[..., None]).reshape(token_count, heads_q * HEAD_SIZE).astype(jnp.bfloat16)
    )
    return result[None]


def solution(mesh):
    placed = (
        P("narrow", "wide", None),
        P(None, "narrow"),
        P(),
        P("narrow", "wide", None),
        P("narrow", "wide", None),
        P("narrow", "wide"),
    )
    return jax.shard_map(
        local, mesh=mesh, in_specs=placed, out_specs=P("narrow", "wide", None), check_vma=False
    )
```

profile of v0, /device:TPU:2, one launch (start us, length us, event | category | flops | bytes accessed | tf_op | source)
XLA Modules:
  0.0 1113.9 jit_solution(16538714596455471011)
XLA Ops:
  6.5 0.7 all-gather.4.cloned.1.call-update
  7.3 0.7 all-gather.6.cloned.1.call-update
  8.8 1.4 reshape_squeeze.3
  10.1 0.9 copy.32
  11.3 116.9 %all-gather.4.cloned.1.call-done = bf16[5120,1024]{1,0:T(8,128)(2,1)} async-done(((bf16[5120,128]{1,0:T(8,128)(2,1)}), bf16[5120,1024]{1,0:T(8,128)(2,1)}) %all-gather.4.cloned.1.call-update) | async-done | bytes 10485776 | tf_op jit(solution)/shard_map/all_gather | solution.py:75
  128.1 5.9 fusion.26
  135.3 0.8 broadcast_select_fusion
  136.1 130.8 %all-gather.6.cloned.1.call-done = bf16[1,1024,1024]{2,1,0:T(8,128)(2,1)} async-done(((bf16[1,16,1024]{2,1,0:T(8,128)(2,1)}), bf16[1,1024,1024]{2,1,0:T(8,128)(2,1)}) %all-gather.6.cloned.1.call-update) | async-done | bytes 2097168 | tf_op jit(solution)/shard_map/all_gather | solution.py:106
  266.9 13.1 %while.15 = (s32[]{:T(128)}, f32[64,4,5]{0,2,1:T(8,128)S(1)}, f32[64,4,5]{0,2,1:T(8,128)S(1)}, f32[64,4,5,128]{3,0,2,1:T(8,128)S(1)}, bf16[2,512,1024]{2,1,0:T(8...) while((s32[]{:T(128)}, f32[64,4,5]{0,2,1:T(8,128)S(1)}, ...), condition=%wide.region_3.4_spmd.clone, body=%wide.region_0.3_spmd.clone.sunk | while | flops 343252736 | bytes 16932996 | solution.py:67
  267.6 0.7 fusion.68
  268.3 1.3 constant_dynamic-slice_fusion.2
  270.2 1.6 bitcast_reduce_fusion.2
  271.8 0.8 fusion.70
  272.6 0.9 fusion.72
  273.5 0.7 dynamic_slice.14
  274.2 0.7 fusion.68
  274.9 1.3 constant_dynamic-slice_fusion.2
  276.8 1.6 bitcast_reduce_fusion.2
  278.4 0.8 fusion.70
  279.1 0.9 fusion.72
  280.1 0.9 reshape.153
  281.0 1.5 fusion.45
  282.4 821.7 %all-reduce.3.cloned.1.call-done = (bf16[64,1024]{1,0:T(8,128)(2,1)}, bf16[64,1024]{1,0:T(8,128)(2,1)}, bf16[64,1024]{1,0:T(8,128)(2,1)}, bf16[64,1024]{1,0:T(8,128)(2,1)}) async-done(((bf16[64,1024]{1,0:T(8,128)(2,1)}, bf16[64,1024]{1,0:T(8,128)(2,1)}, bf16[64,1024]{1,0:T(8,128)(2,1)}, bf16[64,1024]{1,0:T(8,128)(2,1)}), (bf16[64,1024]{1,0:T(8,128)(2,1)}, bf16[64,1024]{1,0:T(8,128)(2,1)}, ...) | async-done | bytes 524304 | tf_op jit(solution)/shard_map/psum | solution.py:16
  1106.3 1.1 convert_element_type.44
  (52 shorter events, 5.5 us)
Async XLA Ops:
  6.5 121.6 %copy-start = (bf16[1,64,5120]{2,1,0:T(8,128)(2,1)S(1)}, bf16[1,64,5120]{2,1,0:T(8,128)(2,1)}, u32[]{:S(2)}) copy-start(bf16[1,64,5120]{2,1,0:T(8,128)(2,1)} %param.8) | copy-start | bytes 1966084
  6.5 121.6 %all-gather.4.cloned.1.call-start = ((), (), s32[]{:S(2)}) async-start(), calls=%async_computation | async-start | bytes 11796480 | tf_op jit(solution)/shard_map/all_gather | solution.py:75
  7.3 259.7 %all-gather.6.cloned.1.call-start = ((), (), s32[]{:S(2)}) async-start(), calls=%async_computation.1 | async-start | bytes 2129920 | tf_op jit(solution)/shard_map/all_gather | solution.py:106
  8.0 1096.1 %all-reduce.3.cloned.1.call-start = ((), (), s32[]{:S(2)}) async-start(), calls=%async_computation.2 | async-start | bytes 1048576 | tf_op jit(solution)/shard_map/psum | solution.py:16
  11.2 123.0 %copy-start.4 = (f32[512]{0:T(512)S(1)}, f32[512]{0:T(512)}, u32[]{:S(2)}) copy-start(f32[512]{0:T(512)} %param.10) | copy-start | bytes 6148
  134.1 132.8 %copy-start.3 = (bf16[64,512]{1,0:T(8,128)(2,1)}, bf16[64,512]{1,0:T(8,128)(2,1)S(1)}, u32[]{:S(2)}) copy-start(bf16[64,512]{1,0:T(8,128)(2,1)S(1)} %slice.44) | copy-start | bytes 196612
  134.5 0.6 copy-start.2
  280.0 824.2 %copy-start.1 = (bf16[64,4,5,128]{3,0,2,1:T(8,128)(2,1)S(1)}, bf16[64,4,5,128]{3,0,2,1:T(8,128)(2,1)}, u32[]{:S(2)}) copy-start(bf16[64,4,5,128]{3,0,2,1:T(8,128)(2,1)} %get-tuple-element.225) | copy-start | bytes 983044
Sparse Core Ops, SparseCore 0:
  9.4 118.7 all-gather.3
  132.5 134.3 all-gather.5
  270.0 834.0 all-reduce.2
where the time goes:
time: 1110 us
  waiting for transfers between devices  1070 us (96%)
  between operations  14 us (1%)
  matrix products  13.7 us (1%)
    psum x1, waiting for transfers between devices, spread(): return lax.psum(jnp.where(mine, value, jnp.zeros_like(value)), axis)  822 us
    all_gather x1, waiting for transfers between devices, local(): lax.all_gather(prefix_kv[0], 'wide', axis=0, tiled=True)  131 us
    all_gather x1, waiting for transfers between devices, local(): lax.all_gather(w_kv, 'narrow', axis=1, tiled=True)  117 us
  transfers between devices with their start and end apart: 3, of which 3 were waited for; matrix products, arithmetic and copies ran while one was open for 2% of the time, Pallas kernels for 0%

commit v1 on v0

v1 whole, which is shorter than its diff:
```python
import functools
import math

import jax
import jax.numpy as jnp
from jax import lax
from jax.experimental import pallas as pl
from jax.experimental.pallas import tpu as pltpu
from jax.sharding import PartitionSpec as P

HEAD = 128
HEADS_KV = 4
GROUP = 5
ROWS = 64
KEY_WIDTH = 512
PREFIX = 1024
SCALE = HEAD ** -0.5 * math.log2(math.e)
NEG = -1e30

FLAT = ("wide", "narrow")


def index_of(y, z, x, c):
    return ((((y // 4) * 8 + z) * 4 + x) * 4 + y % 4) * 2 + c


def move(value, target, only=None):
    pairs = []
    for y in range(8):
        for z in range(8):
            for x in range(4):
                for c in range(2):
                    if only is None or only(y, z, x, c):
                        ty, tz, tx, tc = target(y, z, x, c)
                        pairs.append(
                            (index_of(y, z, x, c), index_of(ty % 8, tz % 8, tx % 4, tc % 2))
                        )
    return lax.ppermute(value, FLAT, pairs)


def along_y(value, s):
    return move(value, lambda y, z, x, c: (y + s, z, x, c))


def along_x(value, s):
    return move(value, lambda y, z, x, c: (y, z, x + s, c))


VM = pl.BlockSpec(memory_space=pltpu.VMEM)
SM = pl.BlockSpec(memory_space=pltpu.SMEM)
PARAMS = pltpu.CompilerParams(vmem_limit_bytes=40 * 1024 * 1024)


def cost(flops, moved, trans=0):
    return pl.CostEstimate(flops=flops, bytes_accessed=moved, transcendentals=trans)


def project_kernel(n, where_ref, *refs):
    rows, (own_ref, other_ref), outs = refs[:n], refs[n : n + 2], refs[n + 2 :]
    core = where_ref[0]
    for row, out in zip(rows, outs):
        for side, w in ((core, own_ref), (1 - core, other_ref)):
            got = jnp.dot(row[...], w[...], preferred_element_type=jnp.float32)
            out[:, pl.ds(pl.multiple_of(side * 128, 128), 128)] = got.astype(jnp.bfloat16)


def project(where, rows, w_own, w_other):
    n = len(rows)
    total = sum(r.shape[0] for r in rows)
    return pl.pallas_call(
        functools.partial(project_kernel, n),
        out_shape=[jax.ShapeDtypeStruct((r.shape[0], 256), jnp.bfloat16) for r in rows],
        in_specs=[SM] + [VM] * (n + 2),
        out_specs=[VM] * n,
        compiler_params=PARAMS,
        cost_estimate=cost(2 * total * 5120 * 256, 5120 * 512 + total * 10240),
    )(where, *rows, w_own, w_other)


def finish_kernel(where_ref, p0, p1, p2a, p2b, p3, gain_ref, cos_ref, sin_ref, out_ref):
    yl = where_ref[1]
    pieces = [
        p0[...].astype(jnp.float32),
        p1[...].astype(jnp.float32),
        jnp.concatenate([p2a[...], p2b[...]], axis=0).astype(jnp.float32),
        p3[...].astype(jnp.float32),
    ]

    def piece(j):
        d = (j - yl) & 3
        return jnp.where(
            d == 0, pieces[0], jnp.where(d == 1, pieces[1], jnp.where(d == 2, pieces[2], pieces[3]))
        )

    keys = jnp.concatenate([piece(0), piece(1)], axis=1)
    meansq = jnp.mean(keys * keys, axis=-1, keepdims=True)
    keys = keys * lax.rsqrt(meansq + 1e-06) * gain_ref[...]
    cosine, sine = cos_ref[...], sin_ref[...]
    for h in range(HEADS_KV):
        k = keys[:, h * HEAD : (h + 1) * HEAD]
        out_ref[:, h * HEAD : (h + 1) * HEAD] = (
            k * cosine + pltpu.roll(k, 64, 1) * sine
        ).astype(jnp.bfloat16)
    out_ref[:, 512:768] = piece(2).astype(jnp.bfloat16)
    out_ref[:, 768:1024] = piece(3).astype(jnp.bfloat16)


def finish(where, pieces, gain, cosine, sine):
    return pl.pallas_call(
        finish_kernel,
        out_shape=jax.ShapeDtypeStruct((ROWS, 1024), jnp.bfloat16),
        in_specs=[SM] + [VM] * 8,
        out_specs=VM,
        compiler_params=PARAMS,
        cost_estimate=cost(64 * 512 * 10, 600000),
    )(where, *pieces, gain, cosine, sine)


def queries(q_ref, g):
    first = g * GROUP
    return jnp.concatenate(
        [q_ref[:, (first + j) * HEAD : (first + j + 1) * HEAD] for j in range(GROUP)], axis=0
    )


def scores(q, k):
    return lax.dot_general(
        q, k, (((1,), (1,)), ((), ())), preferred_element_type=jnp.float32
    ) * SCALE


def prefix_kernel(n, q_ref, *refs):
    blocks, (high_ref, total_ref, sum_ref) = refs[:n], refs[n:]
    for g in range(HEADS_KV):
        q = queries(q_ref, g)
        high = total = acc = None
        for block in blocks:
            s = scores(q, block[:, g * HEAD : (g + 1) * HEAD])
            v = block[:, KEY_WIDTH + g * HEAD : KEY_WIDTH + (g + 1) * HEAD]
            top = jnp.max(s, axis=-1, keepdims=True)
            new = top if high is None else jnp.maximum(high, top)
            p = jnp.exp2(s - new)
            part = jnp.sum(p, axis=-1, keepdims=True)
            pv = jnp.dot(p.astype(jnp.bfloat16), v, preferred_element_type=jnp.float32)
            if high is None:
                total, acc = part, pv
            else:
                factor = jnp.exp2(high - new)
                total, acc = total * factor + part, acc * factor + pv
            high = new
        high_ref[g] = high
        total_ref[g] = total
        sum_ref[g] = acc


def prefix_attend(q, blocks):
    n = len(blocks)
    m = ROWS * GROUP
    keys = sum(b.shape[0] for b in blocks)
    return pl.pallas_call(
        functools.partial(prefix_kernel, n),
        out_shape=[
            jax.ShapeDtypeStruct((HEADS_KV, m, 1), jnp.float32),
            jax.ShapeDtypeStruct((HEADS_KV, m, 1), jnp.float32),
            jax.ShapeDtypeStruct((HEADS_KV, m, HEAD), jnp.float32),
        ],
        in_specs=[VM] * (n + 1),
        out_specs=[VM] * 3,
        compiler_params=PARAMS,
        cost_estimate=cost(4 * 1280 * keys * 128, keys * 2048 + 2000000, 1280 * keys),
    )(q, *blocks)


def last_kernel(where_ref, q_ref, t0, t1, t2, t3, own_ref, high_ref, total_ref, sum_ref, out_ref):
    x, parent = where_ref[2], where_ref[3]
    child = parent >= 0
    d = (parent - x) & 3
    row = lax.broadcasted_iota(jnp.int32, (ROWS, 2 * ROWS), 0)
    col = lax.broadcasted_iota(jnp.int32, (ROWS, 2 * ROWS), 1)
    use = (jnp.where(child, 1, 0) * jnp.where(col < ROWS, 1, 0)) + jnp.where(
        (col >= ROWS) & (col - ROWS <= row), 1, 0
    )
    use = jnp.concatenate([use] * GROUP, axis=0) > 0

    def pick(lo):
        a, b, c, e = (t[:, lo : lo + HEAD].astype(jnp.float32) for t in (t0, t1, t2, t3))
        return jnp.where(d == 0, a, jnp.where(d == 1, b, jnp.where(d == 2, c, e))).astype(
            jnp.bfloat16
        )

    for g in range(HEADS_KV):
        q = queries(q_ref, g)
        lo, hi = g * HEAD, KEY_WIDTH + g * HEAD
        k = jnp.concatenate([pick(lo), own_ref[:, lo : lo + HEAD]], axis=0)
        v = jnp.concatenate([pick(hi), own_ref[:, hi : hi + HEAD]], axis=0)
        s = jnp.where(use, scores(q, k), NEG)
        high = high_ref[g]
        new = jnp.maximum(high, jnp.max(s, axis=-1, keepdims=True))
        p = jnp.exp2(s - new)
        factor = jnp.exp2(high - new)
        total = total_ref[g] * factor + jnp.sum(p, axis=-1, keepdims=True)
        acc = sum_ref[g] * factor + jnp.dot(
            p.astype(jnp.bfloat16), v, preferred_element_type=jnp.float32
        )
        acc = (acc / total).astype(jnp.bfloat16)
        for j in range(GROUP):
            lo = (g * GROUP + j) * HEAD
            out_ref[:, lo : lo + HEAD] = acc[j * ROWS : (j + 1) * ROWS]


def last_attend(where, q, trunks, own, state):
    return pl.pallas_call(
        last_kernel,
        out_shape=jax.ShapeDtypeStruct((ROWS, HEADS_KV * GROUP * HEAD), jnp.bfloat16),
        in_specs=[SM] + [VM] * 9,
        out_specs=VM,
        compiler_params=PARAMS,
        cost_estimate=cost(4 * 1280 * 128 * 128, 3000000, 1280 * 128),
    )(where, q, *trunks, own, *state)


def local(x_branch, w_kv, k_gain, q_branch, prefix_kv, tree_parent):
    wide, narrow = lax.axis_index("wide"), lax.axis_index("narrow")
    yh, z, x = wide // 32, (wide // 4) % 8, wide % 4
    yl, core = narrow // 2, narrow % 2
    parent = tree_parent[0, 0]
    where = jnp.stack([core, yl, x, parent]).astype(jnp.int32)

    rows = x_branch[0]
    half = ROWS // 2
    w_other = move(w_kv, lambda y, z, x, c: (y, z, x, 1 - c))
    below = along_y(rows, 1)
    above = along_y(rows, -1)
    below2 = along_y(below[:half], 1)
    above2 = along_y(above[half:], -1)

    piece = prefix_kv[0]
    piece = jnp.concatenate([piece, along_y(piece, 4)], axis=0)
    for bit in (4, 2, 1):
        got = move(piece, lambda y, z, x, c: (y, z ^ bit, x, c))
        piece = jnp.concatenate([piece, got], axis=0)
    quarter = piece.shape[0] // 2
    left = along_x(piece, 1)
    right = along_x(piece, -1)
    left2 = along_x(left[:quarter], 1)
    right2 = along_x(right[quarter:], -1)
    state = prefix_attend(q_branch[0], [piece, left, right, left2, right2])

    mine, for_below, for_above = project(where, [rows, below, above], w_kv, w_other)
    for_below2, for_above2 = project(where, [below2, above2], w_kv, w_other)
    from_above = along_y(for_below, -1)
    from_below = along_y(for_above, 1)
    from_above2 = along_y(for_below2, -2)
    from_below2 = along_y(for_above2, 2)

    index = jnp.arange(64, dtype=jnp.float32)
    inverse = jnp.exp(-jnp.log(jnp.float32(500000.0)) * 2.0 * index / HEAD)
    inside = jnp.arange(ROWS, dtype=jnp.int32)
    positions = PREFIX + inside + ROWS * (parent >= 0).astype(jnp.int32)
    angle = positions.astype(jnp.float32)[:, None] * inverse[None, :]
    cosine, sine = jnp.cos(angle), jnp.sin(angle)
    cosine = jnp.concatenate([cosine, cosine], axis=1)
    sine = jnp.concatenate([-sine, sine], axis=1)
    own = finish(
        where,
        [mine, from_above, from_above2, from_below2, from_below],
        k_gain[None, :],
        cosine,
        sine,
    )

    root = (yh == 0) & (z == 0)
    first = lambda y, z, x, c: y < 4 and z == 0
    have = jnp.where(root, own, jnp.zeros_like(own))
    have = (
        have
        + move(own, lambda y, z, x, c: (y, 4, x, c), first)
        + move(own, lambda y, z, x, c: (y + 4, 0, x, c), first)
        + move(own, lambda y, z, x, c: (y + 4, 4, x, c), first)
    )
    second = lambda y, z, x, c: z % 4 == 0
    trunk = (
        have
        + move(have, lambda y, z, x, c: (y, z + 1, x, c), second)
        + move(have, lambda y, z, x, c: (y, z - 1, x, c), second)
        + move(have, lambda y, z, x, c: (y, z + 2, x, c), second)
    )
    trunks = [trunk, along_x(trunk, -1), along_x(trunk, 2), along_x(trunk, 1)]
    return last_attend(where, q_branch[0], trunks, own, state)[None]


def solution(mesh):
    placed = (
        P("narrow", "wide", None),
        P(None, "narrow"),
        P(),
        P("narrow", "wide", None),
        P("narrow", "wide", None),
        P("narrow", "wide"),
    )
    return jax.shard_map(
        local, mesh=mesh, in_specs=placed, out_specs=P("narrow", "wide", None), check_vma=False
    )
```

time: 1110 us -> 137 us (0.12)
  the two profiles are of different devices: /device:TPU:2 before, /device:TPU:48 now
where the time goes in v1:
time: 137 us; the launch traced here: 136 us
  starting transfers between devices  79.9 us (58%)
  waiting for transfers between devices  36.6 us (27%)
  Pallas kernels  10.7 us (8%)
  local copies, waits for them, and re-layouts  5.05 us (4%)
  other arithmetic  2.73 us (2%)
    ppermute x26, starting transfers between devices, move(): return lax.ppermute(value, FLAT, pairs)  79.9 us
    ppermute x26, waiting for transfers between devices, move(): return lax.ppermute(value, FLAT, pairs)  36.6 us
    pallas_call x1, Pallas kernels, prefix_attend(): pl.pallas_call(functools.partial(prefix_kernel, n), out_shape=[jax.ShapeD...  3.54 us
    pallas_call x2, Pallas kernels, project(): pl.pallas_call(functools.partial(project_kernel, n), out_shape=[jax.Shape...  3.35 us
    unnamed x12, local copies, waits for them, and re-layouts  3.3 us
    pallas_call x1, Pallas kernels, last_attend(): pl.pallas_call(last_kernel, out_shape=jax.ShapeDtypeStruct((ROWS, HEADS_K...  3.05 us
  transfers between devices with their start and end apart: 26, of which 7 were waited for; matrix products, arithmetic and copies ran while one was open for 6% of the time, Pallas kernels for 6%

profile of v1, /device:TPU:48, one launch (start us, length us, event | category | flops | bytes accessed | tf_op | source)
XLA Modules:
  0.0 136.1 jit_solution(17380357813160195811)
XLA Ops:
  0.0 2.6 %collective-permute-start = (bf16[64,5120]{1,0:T(8,128)(2,1)}, bf16[64,5120]{1,0:T(8,128)(2,1)S(1)}, u32[]{:S(2)}, u32[]{:S(2)}) collective-permute-start(bf16[64,5120]{1,0:T(8,128)(2,1)} %bitcast.12), channel_id=1, source_target_pairs={{0,2},{1,3},{8,10},{9,11},{16,18},{17,19},{24,26},{25,27},{32,34},... | collective-permute-start | bytes 1966088 | tf_op jit(solution)/shard_map/ppermute | solution.py:38
  2.6 3.3 %collective-permute-start.1 = (bf16[64,5120]{1,0:T(8,128)(2,1)}, bf16[64,5120]{1,0:T(8,128)(2,1)S(1)}, u32[]{:S(2)}, u32[]{:S(2)}) collective-permute-start(bf16[64,5120]{1,0:T(8,128)(2,1)} %bitcast.13), channel_id=1, source_target_pairs={{0,262},{1,263},{8,270},{9,271},{16,278},{17,279},{24,286},{25,287... | collective-permute-start | bytes 1966088 | tf_op jit(solution)/shard_map/ppermute | solution.py:38
  7.8 3.8 %collective-permute-start.18 = (bf16[16,1024]{1,0:T(8,128)(2,1)}, bf16[16,1024]{1,0:T(8,128)(2,1)S(1)}, u32[]{:S(2)}, u32[]{:S(2)}) collective-permute-start(bf16[16,1024]{1,0:T(8,128)(2,1)} %bitcast.18), channel_id=1, source_target_pairs={{0,256},{1,257},{8,264},{9,265},{16,272},{17,273},{24,280},{25,281... | collective-permute-start | bytes 98312 | tf_op jit(solution)/shard_map/ppermute | solution.py:38
  12.3 9.3 %collective-permute-done.18 = bf16[16,1024]{1,0:T(8,128)(2,1)S(1)} collective-permute-done((bf16[16,1024]{1,0:T(8,128)(2,1)}, bf16[16,1024]{1,0:T(8,128)(2,1)S(1)}, u32[]{:S(2)}, u32[]{:S(2)}) %collective-permute-start.18) | collective-permute-done | bytes 32800 | tf_op jit(solution)/shard_map/ppermute | solution.py:38
  22.3 10.8 %collective-permute-start.19 = (bf16[32,1024]{1,0:T(8,128)(2,1)S(1)}, bf16[32,1024]{1,0:T(8,128)(2,1)S(1)}, u32[]{:S(2)}, u32[]{:S(2)}) collective-permute-start(bf16[32,1024]{1,0:T(8,128)(2,1)S(1)} %pad_maximum_fusion.2), channel_id=1, source_target_pairs={{0,128},{1,129},{8,136},{9,137},{16,144},{17,145},{24,152},{25,153... | collective-permute-start | bytes 196616 | tf_op jit(solution)/shard_map/ppermute | solution.py:38
  33.3 2.2 %collective-permute-done.19 = bf16[32,1024]{1,0:T(8,128)(2,1)S(1)} collective-permute-done((bf16[32,1024]{1,0:T(8,128)(2,1)S(1)}, bf16[32,1024]{1,0:T(8,128)(2,1)S(1)}, u32[]{:S(2)}, u32[]{:S(2)}) %collective-permute-start.19) | collective-permute-done | bytes 65568 | tf_op jit(solution)/shard_map/ppermute | solution.py:38
  36.4 4.9 %collective-permute-start.20 = (bf16[64,1024]{1,0:T(8,128)(2,1)S(1)}, bf16[64,1024]{1,0:T(8,128)(2,1)S(1)}, u32[]{:S(2)}, u32[]{:S(2)}) collective-permute-start(bf16[64,1024]{1,0:T(8,128)(2,1)S(1)} %pad_maximum_fusion.1), channel_id=1, source_target_pairs={{0,64},{1,65},{8,72},{9,73},{16,80},{17,81},{24,88},{25,89},{32,96... | collective-permute-start | bytes 393224 | tf_op jit(solution)/shard_map/ppermute | solution.py:38
  42.7 2.9 %collective-permute-done.20 = bf16[64,1024]{1,0:T(8,128)(2,1)S(1)} collective-permute-done((bf16[64,1024]{1,0:T(8,128)(2,1)S(1)}, bf16[64,1024]{1,0:T(8,128)(2,1)S(1)}, u32[]{:S(2)}, u32[]{:S(2)}) %collective-permute-start.20) | collective-permute-done | bytes 131104 | tf_op jit(solution)/shard_map/ppermute | solution.py:38
  46.3 2.8 %collective-permute-start.21 = (bf16[128,1024]{1,0:T(8,128)(2,1)S(1)}, bf16[128,1024]{1,0:T(8,128)(2,1)S(1)}, u32[]{:S(2)}, u32[]{:S(2)}) collective-permute-start(bf16[128,1024]{1,0:T(8,128)(2,1)S(1)} %pad_maximum_fusion), channel_id=1, source_target_pairs={{0,32},{1,33},{8,40},{9,41},{16,48},{17,49},{24,56},{25,57},{32,0}... | collective-permute-start | bytes 786440 | tf_op jit(solution)/shard_map/ppermute | solution.py:38
  49.8 5.6 %collective-permute-start.4 = (bf16[32,5120]{1,0:T(8,128)(2,1)S(1)}, bf16[32,5120]{1,0:T(8,128)(2,1)S(1)}, u32[]{:S(2)}, u32[]{:S(2)}) collective-permute-start(bf16[32,5120]{1,0:T(8,128)(2,1)S(1)} %slice.16), channel_id=1, source_target_pairs={{0,2},{1,3},{8,10},{9,11},{16,18},{17,19},{24,26},{25,27},{32,34},... | collective-permute-start | bytes 983048 | tf_op jit(solution)/shard_map/ppermute | solution.py:38
  59.4 3.5 %collective-permute-start.22 = (bf16[256,1024]{1,0:T(8,128)(2,1)}, bf16[256,1024]{1,0:T(8,128)(2,1)S(1)}, u32[]{:S(2)}, u32[]{:S(2)}) collective-permute-start(bf16[256,1024]{1,0:T(8,128)(2,1)} %constant_dynamic-update-slice_fusion.refs_0_), channel_id=1, source_target_pairs={{0,8},{1,9},{8,16},{9,17},{16,24},{17,25},{24,0},{25,1},{32,40},{3... | collective-permute-start | bytes 1572872 | tf_op jit(solution)/shard_map/ppermute | solution.py:38
  62.9 3.7 %collective-permute-start.23 = (bf16[256,1024]{1,0:T(8,128)(2,1)}, bf16[256,1024]{1,0:T(8,128)(2,1)}, u32[]{:S(2)}, u32[]{:S(2)}) collective-permute-start(bf16[256,1024]{1,0:T(8,128)(2,1)} %constant_dynamic-update-slice_fusion.refs_0_), channel_id=1, source_target_pairs={{0,24},{1,25},{8,0},{9,1},{16,8},{17,9},{24,16},{25,17},{32,56},{3... | collective-permute-start | bytes 1572872 | tf_op jit(solution)/shard_map/ppermute | solution.py:38
  68.1 4.1 %collective-permute-start.6 = (bf16[32,256]{1,0:T(8,128)(2,1)S(1)}, bf16[32,256]{1,0:T(8,128)(2,1)S(1)}, u32[]{:S(2)}, u32[]{:S(2)}) collective-permute-start(bf16[32,256]{1,0:T(8,128)(2,1)S(1)} %get-tuple-element.15), channel_id=1, source_target_pairs={{0,260},{1,261},{8,268},{9,269},{16,276},{17,277},{24,284},{25,285... | collective-permute-start | bytes 49160 | tf_op jit(solution)/shard_map/ppermute | solution.py:38
  74.2 3.9 %collective-permute-start.3 = (bf16[64,256]{1,0:T(8,128)(2,1)S(1)}, bf16[64,256]{1,0:T(8,128)(2,1)S(1)}, u32[]{:S(2)}, u32[]{:S(2)}) collective-permute-start(bf16[64,256]{1,0:T(8,128)(2,1)S(1)} %get-tuple-element.14), channel_id=1, source_target_pairs={{0,262},{1,263},{8,270},{9,271},{16,278},{17,279},{24,286},{25,287... | collective-permute-start | bytes 98312 | tf_op jit(solution)/shard_map/ppermute | solution.py:38
  78.1 2.4 %collective-permute-start.7 = (bf16[32,256]{1,0:T(8,128)(2,1)S(1)}, bf16[32,256]{1,0:T(8,128)(2,1)S(1)}, u32[]{:S(2)}, u32[]{:S(2)}) collective-permute-start(bf16[32,256]{1,0:T(8,128)(2,1)S(1)} %get-tuple-element.16), channel_id=1, source_target_pairs={{0,4},{1,5},{8,12},{9,13},{16,20},{17,21},{24,28},{25,29},{32,36},... | collective-permute-start | bytes 49160 | tf_op jit(solution)/shard_map/ppermute | solution.py:38
  80.5 3.4 %collective-permute-start.8 = (bf16[64,256]{1,0:T(8,128)(2,1)S(1)}, bf16[64,256]{1,0:T(8,128)(2,1)S(1)}, u32[]{:S(2)}, u32[]{:S(2)}) collective-permute-start(bf16[64,256]{1,0:T(8,128)(2,1)S(1)} %get-tuple-element.17), channel_id=1, source_target_pairs={{0,2},{1,3},{8,10},{9,11},{16,18},{17,19},{24,26},{25,27},{32,34},... | collective-permute-start | bytes 98312 | tf_op jit(solution)/shard_map/ppermute | solution.py:38
  89.8 17.8 %collective-permute-done.10 = bf16[64,1024]{1,0:T(8,128)(2,1)S(1)} collective-permute-done((bf16[64,1024]{1,0:T(8,128)(2,1)S(1)}, bf16[64,1024]{1,0:T(8,128)(2,1)S(1)}, u32[]{:S(2)}, u32[]{:S(2)}) %collective-permute-start.10) | collective-permute-done | bytes 131104 | tf_op jit(solution)/shard_map/ppermute | solution.py:38
  111.6 2.2 %collective-permute-start.24 = (bf16[128,1024]{1,0:T(8,128)(2,1)S(1)}, bf16[128,1024]{1,0:T(8,128)(2,1)S(1)}, u32[]{:S(2)}, u32[]{:S(2)}) collective-permute-start(bf16[128,1024]{1,0:T(8,128)(2,1)S(1)} %slice.18), channel_id=1, source_target_pairs={{0,8},{1,9},{8,16},{9,17},{16,24},{17,25},{24,0},{25,1},{32,40},{3... | collective-permute-start | bytes 786440 | tf_op jit(solution)/shard_map/ppermute | solution.py:38
  114.8 4.9 %collective-permute-start.25 = (bf16[128,1024]{1,0:T(8,128)(2,1)S(1)}, bf16[128,1024]{1,0:T(8,128)(2,1)S(1)}, u32[]{:S(2)}, u32[]{:S(2)}) collective-permute-start(bf16[128,1024]{1,0:T(8,128)(2,1)S(1)} %slice.19), channel_id=1, source_target_pairs={{0,24},{1,25},{8,0},{9,1},{16,8},{17,9},{24,16},{25,17},{32,56},{3... | collective-permute-start | bytes 786440 | tf_op jit(solution)/shard_map/ppermute | solution.py:38
  119.7 2.2 %collective-permute-start.15 = (bf16[64,1024]{1,0:T(8,128)(2,1)S(1)}, bf16[64,1024]{1,0:T(8,128)(2,1)S(1)}, u32[]{:S(2)}, u32[]{:S(2)}) collective-permute-start(bf16[64,1024]{1,0:T(8,128)(2,1)S(1)} %add_add_fusion.t0), channel_id=1, source_target_pairs={{0,24},{1,25},{8,0},{9,1},{16,8},{17,9},{24,16},{25,17},{32,56},{3... | collective-permute-start | bytes 393224 | tf_op jit(solution)/shard_map/ppermute | solution.py:38
  122.0 2.7 %collective-permute-start.16 = (bf16[64,1024]{1,0:T(8,128)(2,1)S(1)}, bf16[64,1024]{1,0:T(8,128)(2,1)S(1)}, u32[]{:S(2)}, u32[]{:S(2)}) collective-permute-start(bf16[64,1024]{1,0:T(8,128)(2,1)S(1)} %add_add_fusion.t0), channel_id=1, source_target_pairs={{0,16},{1,17},{8,24},{9,25},{16,0},{17,1},{24,8},{25,9},{32,48},{3... | collective-permute-start | bytes 393224 | tf_op jit(solution)/shard_map/ppermute | solution.py:38
  124.7 2.8 %collective-permute-start.17 = (bf16[64,1024]{1,0:T(8,128)(2,1)S(1)}, bf16[64,1024]{1,0:T(8,128)(2,1)S(1)}, u32[]{:S(2)}, u32[]{:S(2)}) collective-permute-start(bf16[64,1024]{1,0:T(8,128)(2,1)S(1)} %add_add_fusion.t0), channel_id=1, source_target_pairs={{0,8},{1,9},{8,16},{9,17},{16,24},{17,25},{24,0},{25,1},{32,40},{3... | collective-permute-start | bytes 393224 | tf_op jit(solution)/shard_map/ppermute | solution.py:38
  127.5 3.5 %shard_map.67 = (f32[4,320,1]{2,1,0:T(8,128)S(1)}, f32[4,320,1]{2,1,0:T(8,128)S(1)}, f32[4,320,128]{2,1,0:T(8,128)S(1)}) custom-call(bf16[64,2560]{1,0:T(8,128)(2,1)S(1)} %bitcast.15, bf16[256,1024]{1,0:T(8,128)(2,1)} %constant_dynamic-update-slice_fusion.refs_0_, bf16[256,1024]{1,0:T(8,128)(2,1)S(1)} %collective-permute-done.22.refs_1_, ...), custom_call_target="tpu_custom_call" | custom-call | flops 671088640 | bytes 4097152 | tf_op jit(solution)/shard_map/pallas_call | solution.py:160
  133.1 3.1 %shard_map.68 = bf16[64,2560]{1,0:T(8,128)(2,1)} custom-call(s32[4]{0:T(128)S(1)} %pad_add_fusion.where_ref, bf16[64,2560]{1,0:T(8,128)(2,1)S(1)} %bitcast.16, bf16[64,1024]{1,0:T(8,128)(2,1)S(1)} %add_add_fusion.t0, bf16[64,1024]{1,0:T(8,128)(2,1)S(1)} %collective-permute-done.15.t1, bf16[64,1024]{1,0:T(8,128)(2,1)S(1)} %collective-permute-done.16.t2, ...), custom_call_target="tpu_custom_call" | custom-call | flops 83886080 | bytes 3000000 | tf_op jit(solution)/shard_map/pallas_call | solution.py:212
  (60 shorter events, 26.6 us)
Async XLA Ops:
  0.0 49.8 %collective-permute-start = (bf16[64,5120]{1,0:T(8,128)(2,1)}, bf16[64,5120]{1,0:T(8,128)(2,1)S(1)}, u32[]{:S(2)}, u32[]{:S(2)}) collective-permute-start(bf16[64,5120]{1,0:T(8,128)(2,1)} %bitcast.12), channel_id=1, source_target_pairs={{0,2},{1,3},{8,10},{9,11},{16,18},{17,19},{24,26},{25,27},{32,34},... | collective-permute-start | bytes 1966088 | tf_op jit(solution)/shard_map/ppermute | solution.py:38
  2.6 52.8 %collective-permute-start.1 = (bf16[64,5120]{1,0:T(8,128)(2,1)}, bf16[64,5120]{1,0:T(8,128)(2,1)S(1)}, u32[]{:S(2)}, u32[]{:S(2)}) collective-permute-start(bf16[64,5120]{1,0:T(8,128)(2,1)} %bitcast.13), channel_id=1, source_target_pairs={{0,262},{1,263},{8,270},{9,271},{16,278},{17,279},{24,286},{25,287... | collective-permute-start | bytes 1966088 | tf_op jit(solution)/shard_map/ppermute | solution.py:38
  5.9 60.8 %collective-permute-start.2 = (bf16[5120,128]{1,0:T(8,128)(2,1)}, bf16[5120,128]{1,0:T(8,128)(2,1)S(1)}, u32[]{:S(2)}, u32[]{:S(2)}) collective-permute-start(bf16[5120,128]{1,0:T(8,128)(2,1)} %refs_2_.1), channel_id=1, source_target_pairs={{0,1},{1,0},{8,9},{9,8},{16,17},{17,16},{24,25},{25,24},{32,33},{3... | collective-permute-start | bytes 3932168 | tf_op jit(solution)/shard_map/ppermute | solution.py:38
  7.8 13.8 %collective-permute-start.18 = (bf16[16,1024]{1,0:T(8,128)(2,1)}, bf16[16,1024]{1,0:T(8,128)(2,1)S(1)}, u32[]{:S(2)}, u32[]{:S(2)}) collective-permute-start(bf16[16,1024]{1,0:T(8,128)(2,1)} %bitcast.18), channel_id=1, source_target_pairs={{0,256},{1,257},{8,264},{9,265},{16,272},{17,273},{24,280},{25,281... | collective-permute-start | bytes 98312 | tf_op jit(solution)/shard_map/ppermute | solution.py:38
  22.3 13.3 %collective-permute-start.19 = (bf16[32,1024]{1,0:T(8,128)(2,1)S(1)}, bf16[32,1024]{1,0:T(8,128)(2,1)S(1)}, u32[]{:S(2)}, u32[]{:S(2)}) collective-permute-start(bf16[32,1024]{1,0:T(8,128)(2,1)S(1)} %pad_maximum_fusion.2), channel_id=1, source_target_pairs={{0,128},{1,129},{8,136},{9,137},{16,144},{17,145},{24,152},{25,153... | collective-permute-start | bytes 196616 | tf_op jit(solution)/shard_map/ppermute | solution.py:38
  36.4 9.2 %collective-permute-start.20 = (bf16[64,1024]{1,0:T(8,128)(2,1)S(1)}, bf16[64,1024]{1,0:T(8,128)(2,1)S(1)}, u32[]{:S(2)}, u32[]{:S(2)}) collective-permute-start(bf16[64,1024]{1,0:T(8,128)(2,1)S(1)} %pad_maximum_fusion.1), channel_id=1, source_target_pairs={{0,64},{1,65},{8,72},{9,73},{16,80},{17,81},{24,88},{25,89},{32,96... | collective-permute-start | bytes 393224 | tf_op jit(solution)/shard_map/ppermute | solution.py:38
  46.3 12.3 %collective-permute-start.21 = (bf16[128,1024]{1,0:T(8,128)(2,1)S(1)}, bf16[128,1024]{1,0:T(8,128)(2,1)S(1)}, u32[]{:S(2)}, u32[]{:S(2)}) collective-permute-start(bf16[128,1024]{1,0:T(8,128)(2,1)S(1)} %pad_maximum_fusion), channel_id=1, source_target_pairs={{0,32},{1,33},{8,40},{9,41},{16,48},{17,49},{24,56},{25,57},{32,0}... | collective-permute-start | bytes 786440 | tf_op jit(solution)/shard_map/ppermute | solution.py:38
  49.8 16.8 %collective-permute-start.4 = (bf16[32,5120]{1,0:T(8,128)(2,1)S(1)}, bf16[32,5120]{1,0:T(8,128)(2,1)S(1)}, u32[]{:S(2)}, u32[]{:S(2)}) collective-permute-start(bf16[32,5120]{1,0:T(8,128)(2,1)S(1)} %slice.16), channel_id=1, source_target_pairs={{0,2},{1,3},{8,10},{9,11},{16,18},{17,19},{24,26},{25,27},{32,34},... | collective-permute-start | bytes 983048 | tf_op jit(solution)/shard_map/ppermute | solution.py:38
  55.5 11.1 %collective-permute-start.5 = (bf16[32,5120]{1,0:T(8,128)(2,1)S(1)}, bf16[32,5120]{1,0:T(8,128)(2,1)S(1)}, u32[]{:S(2)}, u32[]{:S(2)}) collective-permute-start(bf16[32,5120]{1,0:T(8,128)(2,1)S(1)} %slice.17), channel_id=1, source_target_pairs={{0,262},{1,263},{8,270},{9,271},{16,278},{17,279},{24,286},{25,287... | collective-permute-start | bytes 983048 | tf_op jit(solution)/shard_map/ppermute | solution.py:38
  59.4 52.1 %collective-permute-start.22 = (bf16[256,1024]{1,0:T(8,128)(2,1)}, bf16[256,1024]{1,0:T(8,128)(2,1)S(1)}, u32[]{:S(2)}, u32[]{:S(2)}) collective-permute-start(bf16[256,1024]{1,0:T(8,128)(2,1)} %constant_dynamic-update-slice_fusion.refs_0_), channel_id=1, source_target_pairs={{0,8},{1,9},{8,16},{9,17},{16,24},{17,25},{24,0},{25,1},{32,40},{3... | collective-permute-start | bytes 1572872 | tf_op jit(solution)/shard_map/ppermute | solution.py:38
  62.9 50.9 %collective-permute-start.23 = (bf16[256,1024]{1,0:T(8,128)(2,1)}, bf16[256,1024]{1,0:T(8,128)(2,1)}, u32[]{:S(2)}, u32[]{:S(2)}) collective-permute-start(bf16[256,1024]{1,0:T(8,128)(2,1)} %constant_dynamic-update-slice_fusion.refs_0_), channel_id=1, source_target_pairs={{0,24},{1,25},{8,0},{9,1},{16,8},{17,9},{24,16},{25,17},{32,56},{3... | collective-permute-start | bytes 1572872 | tf_op jit(solution)/shard_map/ppermute | solution.py:38
  68.1 12.4 %collective-permute-start.6 = (bf16[32,256]{1,0:T(8,128)(2,1)S(1)}, bf16[32,256]{1,0:T(8,128)(2,1)S(1)}, u32[]{:S(2)}, u32[]{:S(2)}) collective-permute-start(bf16[32,256]{1,0:T(8,128)(2,1)S(1)} %get-tuple-element.15), channel_id=1, source_target_pairs={{0,260},{1,261},{8,268},{9,269},{16,276},{17,277},{24,284},{25,285... | collective-permute-start | bytes 49160 | tf_op jit(solution)/shard_map/ppermute | solution.py:38
  74.2 10.5 %collective-permute-start.3 = (bf16[64,256]{1,0:T(8,128)(2,1)S(1)}, bf16[64,256]{1,0:T(8,128)(2,1)S(1)}, u32[]{:S(2)}, u32[]{:S(2)}) collective-permute-start(bf16[64,256]{1,0:T(8,128)(2,1)S(1)} %get-tuple-element.14), channel_id=1, source_target_pairs={{0,262},{1,263},{8,270},{9,271},{16,278},{17,279},{24,286},{25,287... | collective-permute-start | bytes 98312 | tf_op jit(solution)/shard_map/ppermute | solution.py:38
  78.1 6.5 %collective-permute-start.7 = (bf16[32,256]{1,0:T(8,128)(2,1)S(1)}, bf16[32,256]{1,0:T(8,128)(2,1)S(1)}, u32[]{:S(2)}, u32[]{:S(2)}) collective-permute-start(bf16[32,256]{1,0:T(8,128)(2,1)S(1)} %get-tuple-element.16), channel_id=1, source_target_pairs={{0,4},{1,5},{8,12},{9,13},{16,20},{17,21},{24,28},{25,29},{32,36},... | collective-permute-start | bytes 49160 | tf_op jit(solution)/shard_map/ppermute | solution.py:38
  87.7 19.8 %collective-permute-start.10 = (bf16[64,1024]{1,0:T(8,128)(2,1)S(1)}, bf16[64,1024]{1,0:T(8,128)(2,1)S(1)}, u32[]{:S(2)}, u32[]{:S(2)}) collective-permute-start(bf16[64,1024]{1,0:T(8,128)(2,1)S(1)} %shard_map.66.own_ref), channel_id=1, source_target_pairs={{0,256},{1,257},{8,264},{9,265},{16,272},{17,273},{24,280},{25,281... | collective-permute-start | bytes 393224 | tf_op jit(solution)/shard_map/ppermute | solution.py:38
  89.0 18.6 %collective-permute-start.9 = (bf16[64,1024]{1,0:T(8,128)(2,1)S(1)}, bf16[64,1024]{1,0:T(8,128)(2,1)S(1)}, u32[]{:S(2)}, u32[]{:S(2)}) collective-permute-start(bf16[64,1024]{1,0:T(8,128)(2,1)S(1)} %shard_map.66.own_ref), channel_id=1, source_target_pairs={{0,128},{1,129},{8,136},{9,137},{16,144},{17,145},{24,152},{25,153... | collective-permute-start | bytes 393224 | tf_op jit(solution)/shard_map/ppermute | solution.py:38
  107.6 12.0 %collective-permute-start.14 = (bf16[64,1024]{1,0:T(8,128)(2,1)S(1)}, bf16[64,1024]{1,0:T(8,128)(2,1)S(1)}, u32[]{:S(2)}, u32[]{:S(2)}) collective-permute-start(bf16[64,1024]{1,0:T(8,128)(2,1)S(1)} %add_add_fusion.1), channel_id=1, source_target_pairs={{0,64},{1,65},{8,72},{9,73},{16,80},{17,81},{24,88},{25,89},{128,1... | collective-permute-start | bytes 393224 | tf_op jit(solution)/shard_map/ppermute | solution.py:38
  108.9 10.7 %collective-permute-start.13 = (bf16[64,1024]{1,0:T(8,128)(2,1)S(1)}, bf16[64,1024]{1,0:T(8,128)(2,1)S(1)}, u32[]{:S(2)}, u32[]{:S(2)}) collective-permute-start(bf16[64,1024]{1,0:T(8,128)(2,1)S(1)} %add_add_fusion.1), channel_id=1, source_target_pairs={{0,224},{1,225},{8,232},{9,233},{16,240},{17,241},{24,248},{25,249... | collective-permute-start | bytes 393224 | tf_op jit(solution)/shard_map/ppermute | solution.py:38
  110.2 9.4 %collective-permute-start.12 = (bf16[64,1024]{1,0:T(8,128)(2,1)S(1)}, bf16[64,1024]{1,0:T(8,128)(2,1)S(1)}, u32[]{:S(2)}, u32[]{:S(2)}) collective-permute-start(bf16[64,1024]{1,0:T(8,128)(2,1)S(1)} %add_add_fusion.1), channel_id=1, source_target_pairs={{0,32},{1,33},{8,40},{9,41},{16,48},{17,49},{24,56},{25,57},{128,1... | collective-permute-start | bytes 393224 | tf_op jit(solution)/shard_map/ppermute | solution.py:38
  111.6 15.9 %collective-permute-start.24 = (bf16[128,1024]{1,0:T(8,128)(2,1)S(1)}, bf16[128,1024]{1,0:T(8,128)(2,1)S(1)}, u32[]{:S(2)}, u32[]{:S(2)}) collective-permute-start(bf16[128,1024]{1,0:T(8,128)(2,1)S(1)} %slice.18), channel_id=1, source_target_pairs={{0,8},{1,9},{8,16},{9,17},{16,24},{17,25},{24,0},{25,1},{32,40},{3... | collective-permute-start | bytes 786440 | tf_op jit(solution)/shard_map/ppermute | solution.py:38
  114.8 12.7 %collective-permute-start.25 = (bf16[128,1024]{1,0:T(8,128)(2,1)S(1)}, bf16[128,1024]{1,0:T(8,128)(2,1)S(1)}, u32[]{:S(2)}, u32[]{:S(2)}) collective-permute-start(bf16[128,1024]{1,0:T(8,128)(2,1)S(1)} %slice.19), channel_id=1, source_target_pairs={{0,24},{1,25},{8,0},{9,1},{16,8},{17,9},{24,16},{25,17},{32,56},{3... | collective-permute-start | bytes 786440 | tf_op jit(solution)/shard_map/ppermute | solution.py:38
  119.7 11.4 %collective-permute-start.15 = (bf16[64,1024]{1,0:T(8,128)(2,1)S(1)}, bf16[64,1024]{1,0:T(8,128)(2,1)S(1)}, u32[]{:S(2)}, u32[]{:S(2)}) collective-permute-start(bf16[64,1024]{1,0:T(8,128)(2,1)S(1)} %add_add_fusion.t0), channel_id=1, source_target_pairs={{0,24},{1,25},{8,0},{9,1},{16,8},{17,9},{24,16},{25,17},{32,56},{3... | collective-permute-start | bytes 393224 | tf_op jit(solution)/shard_map/ppermute | solution.py:38
  122.0 9.1 %collective-permute-start.16 = (bf16[64,1024]{1,0:T(8,128)(2,1)S(1)}, bf16[64,1024]{1,0:T(8,128)(2,1)S(1)}, u32[]{:S(2)}, u32[]{:S(2)}) collective-permute-start(bf16[64,1024]{1,0:T(8,128)(2,1)S(1)} %add_add_fusion.t0), channel_id=1, source_target_pairs={{0,16},{1,17},{8,24},{9,25},{16,0},{17,1},{24,8},{25,9},{32,48},{3... | collective-permute-start | bytes 393224 | tf_op jit(solution)/shard_map/ppermute | solution.py:38
  124.7 8.4 %collective-permute-start.17 = (bf16[64,1024]{1,0:T(8,128)(2,1)S(1)}, bf16[64,1024]{1,0:T(8,128)(2,1)S(1)}, u32[]{:S(2)}, u32[]{:S(2)}) collective-permute-start(bf16[64,1024]{1,0:T(8,128)(2,1)S(1)} %add_add_fusion.t0), channel_id=1, source_target_pairs={{0,8},{1,9},{8,16},{9,17},{16,24},{17,25},{24,0},{25,1},{32,40},{3... | collective-permute-start | bytes 393224 | tf_op jit(solution)/shard_map/ppermute | solution.py:38
  (6 other events, 104.7 us)

commit v2 on v1

v2 whole, which is shorter than its diff:
```python
import functools
import math

import jax
import jax.numpy as jnp
from jax import lax
from jax.experimental import pallas as pl
from jax.experimental.pallas import tpu as pltpu
from jax.sharding import PartitionSpec as P

HEAD = 128
HEADS_KV = 4
GROUP = 5
ROWS = 64
KEY_WIDTH = 512
PREFIX = 1024
SCALE = HEAD ** -0.5 * math.log2(math.e)
NEG = -1e30

PARTS = ("yh", "z", "x", "yl", "core")
SIZES = (2, 8, 4, 4, 2)
WIDE, NARROW = PARTS[:3], PARTS[3:]
Y = ("yh", "yl")


NEXT_A = [(i, i ^ 1) for i in range(8)]
NEXT_B = [(i, (i + (1 if i % 2 else -1)) % 8) for i in range(8)]


X_NEXT_A = [(i, i ^ 1) for i in range(4)]
X_NEXT_B = [(i, 3 - i) for i in range(4)]


def ring_x(value, pairs):
    return lax.ppermute(value, "x", pairs)


def along_x(value, s):
    return lax.ppermute(value, "x", [(i, (i + s) % 4) for i in range(4)])


def along_y(value, pairs):
    return lax.ppermute(value, Y, pairs)


def along_z(value, bit):
    return lax.ppermute(value, "z", [(i, i ^ bit) for i in range(8)])


def swap(value):
    return lax.ppermute(value, "core", [(0, 1), (1, 0)])


def along_yh_z(value, pairs):
    return lax.ppermute(value, ("yh", "z"), [(a * 8 + b, c * 8 + d) for a, b, c, d in pairs])


VM = pl.BlockSpec(memory_space=pltpu.VMEM)
SM = pl.BlockSpec(memory_space=pltpu.SMEM)
PARAMS = pltpu.CompilerParams(vmem_limit_bytes=40 * 1024 * 1024)


def cost(flops, moved, trans=0):
    return pl.CostEstimate(flops=flops, bytes_accessed=moved, transcendentals=trans)


ANY = pl.BlockSpec(memory_space=pl.ANY)
DEPTH = 5120
HALF = DEPTH // 2


def join_kernel(n, *refs):
    parts, out_ref = refs[:n], refs[-1]
    at = 0
    for part in parts:
        out_ref[at : at + part.shape[0]] = part[...]
        at += part.shape[0]


def join(parts, after=()):
    n = len(parts)
    total = sum(p.shape[0] for p in parts)
    width = parts[0].shape[1]
    return pl.pallas_call(
        functools.partial(join_kernel, n),
        out_shape=jax.ShapeDtypeStruct((total, width), parts[0].dtype),
        in_specs=[VM] * n + [ANY] * len(after),
        out_specs=VM,
        compiler_params=PARAMS,
        cost_estimate=cost(0, 4 * total * width),
    )(*parts, *after)


def pack_kernel(rows_ref, w_ref, after_ref, for_a_ref, for_b_ref):
    for_b_ref[:HALF] = w_ref[:HALF]
    for_a_ref[:HALF] = w_ref[HALF:]
    for i in range(HALF // 128):
        at = HALF + i * ROWS
        for_a_ref[at : at + ROWS] = rows_ref[:, i * 128 : (i + 1) * 128]
        for_b_ref[at : at + ROWS] = rows_ref[:, HALF + i * 128 : HALF + (i + 1) * 128]


def pack(rows, w, after):
    out = jax.ShapeDtypeStruct((HALF + HALF // 128 * ROWS, 128), rows.dtype)
    return pl.pallas_call(
        pack_kernel,
        out_shape=[out, out],
        in_specs=[VM, VM, ANY],
        out_specs=[VM] * 2,
        compiler_params=PARAMS,
        cost_estimate=cost(0, 4 * (rows.size + w.size)),
    )(rows, w, after)


def weights_kernel(from_a_ref, from_b_ref, piece_ref, q_ref, out_ref):
    out_ref[:HALF] = from_b_ref[:HALF]
    out_ref[HALF:] = from_a_ref[:HALF]


def weights(from_a, from_b, *after):
    return pl.pallas_call(
        weights_kernel,
        out_shape=jax.ShapeDtypeStruct((DEPTH, 128), from_a.dtype),
        in_specs=[VM, VM, ANY, ANY],
        out_specs=VM,
        compiler_params=PARAMS,
        cost_estimate=cost(0, 4 * DEPTH * 128),
    )(from_a, from_b, *after)


def project_kernel(
    where_ref, rows, own, other, from_a, from_b, came_other, local_ref, to_a_ref, to_b_ref
):
    first = where_ref[0] == 0

    def product(at, far, near):
        acc = None
        for k in range(0, HALF, 512):
            blocks = [HALF + (k // 128 + i) * ROWS for i in range(4)]
            x = jnp.concatenate([far[b : b + ROWS] for b in blocks], axis=1)
            x = jnp.concatenate([rows[:, at + k : at + k + 512], x], axis=0)
            w = jnp.concatenate(
                [
                    own[at + k : at + k + 512],
                    other[at + k : at + k + 512],
                    near[k : k + 512],
                    came_other[at + k : at + k + 512],
                ],
                axis=1,
            )
            got = jnp.dot(x, w, preferred_element_type=jnp.float32)
            acc = got if acc is None else acc + got
        a, b, c, d = (acc[:, i * 128 : (i + 1) * 128] for i in range(4))
        return jnp.concatenate(
            [
                jnp.where(first, a, b),
                jnp.where(first, b, a),
                jnp.where(first, c, d),
                jnp.where(first, d, c),
            ],
            axis=1,
        )

    one = product(0, from_a, from_b)
    two = product(HALF, from_b, from_a)
    local_ref[:, :256] = one[:ROWS, :256] + two[:ROWS, :256]
    local_ref[:, 256:512] = two[:ROWS, 256:]
    local_ref[:, 512:] = one[:ROWS, 256:]
    to_a_ref[...] = one[ROWS:].astype(jnp.bfloat16)
    to_b_ref[...] = two[ROWS:].astype(jnp.bfloat16)


def project(where, *arrays):
    back = jax.ShapeDtypeStruct((ROWS, 512), jnp.bfloat16)
    return pl.pallas_call(
        project_kernel,
        out_shape=[jax.ShapeDtypeStruct((ROWS, 768), jnp.float32), back, back],
        in_specs=[SM] + [VM] * 6,
        out_specs=[VM] * 3,
        compiler_params=PARAMS,
        cost_estimate=cost(4 * 2 * ROWS * HALF * 512, 7000000),
    )(where, *arrays)


def finish_kernel(where_ref, local_ref, got_a, got_b, gain_ref, cos_ref, sin_ref, out_ref, piece_ref):
    y = where_ref[1]
    even = (y & 1) == 0
    a = got_a[:, :256].astype(jnp.float32) + local_ref[:, 256:512]
    b = got_b[:, :256].astype(jnp.float32) + local_ref[:, 512:]
    piece_ref[0] = local_ref[:, :256]
    piece_ref[1] = jnp.where(even, a, b)
    piece_ref[2] = got_a[:, 256:].astype(jnp.float32) + got_b[:, 256:].astype(jnp.float32)
    piece_ref[3] = jnp.where(even, b, a)
    a, b, c, d = (piece_ref[(j - y) & 3] for j in range(4))
    keys = jnp.concatenate([a, b], axis=1)
    meansq = jnp.mean(keys * keys, axis=-1, keepdims=True)
    keys = keys * lax.rsqrt(meansq + 1e-06) * gain_ref[...]
    cosine, sine = cos_ref[...], sin_ref[...]
    for h in range(HEADS_KV):
        k = keys[:, h * HEAD : (h + 1) * HEAD]
        out_ref[:, h * HEAD : (h + 1) * HEAD] = (
            k * cosine + pltpu.roll(k, 64, 1) * sine
        ).astype(jnp.bfloat16)
    out_ref[:, 512:768] = c.astype(jnp.bfloat16)
    out_ref[:, 768:1024] = d.astype(jnp.bfloat16)


def finish(where, here, got_a, got_b, gain, cosine, sine):
    return pl.pallas_call(
        finish_kernel,
        out_shape=jax.ShapeDtypeStruct((ROWS, 1024), jnp.bfloat16),
        in_specs=[SM] + [VM] * 6,
        out_specs=VM,
        scratch_shapes=[pltpu.VMEM((4, ROWS, 256), jnp.float32)],
        compiler_params=PARAMS,
        cost_estimate=cost(64 * 512 * 10, 600000),
    )(where, here, got_a, got_b, gain, cosine, sine)


def queries(q_ref, g):
    first = g * GROUP
    return jnp.concatenate(
        [q_ref[:, (first + j) * HEAD : (first + j + 1) * HEAD] for j in range(GROUP)], axis=0
    )


def scores(q, k):
    return lax.dot_general(
        q, k, (((1,), (1,)), ((), ())), preferred_element_type=jnp.float32
    ) * SCALE


def prefix_kernel(n, q_ref, q2_ref, *refs):
    blocks, (high_ref, total_ref, sum_ref, send_ref) = refs[:n], refs[-4:]
    lane = lax.broadcasted_iota(jnp.int32, (ROWS, HEAD), 1)
    logs = jnp.zeros((ROWS, HEAD), jnp.float32)

    def attend(q, g):
        high = total = acc = None
        for block in blocks:
            s = scores(q, block[:, g * HEAD : (g + 1) * HEAD])
            v = block[:, KEY_WIDTH + g * HEAD : KEY_WIDTH + (g + 1) * HEAD]
            top = jnp.max(s, axis=-1, keepdims=True)
            new = top if high is None else jnp.maximum(high, top)
            p = jnp.exp2(s - new)
            part = jnp.sum(p, axis=-1, keepdims=True)
            pv = jnp.dot(p.astype(jnp.bfloat16), v, preferred_element_type=jnp.float32)
            if high is None:
                total, acc = part, pv
            else:
                factor = jnp.exp2(high - new)
                total, acc = total * factor + part, acc * factor + pv
            high = new
        return high, total, acc

    for g in range(HEADS_KV):
        high, total, acc = attend(queries(q2_ref, g), g)
        acc = (acc / total).astype(jnp.bfloat16)
        log = high + jnp.log2(total)
        for j in range(GROUP):
            h = g * GROUP + j
            send_ref[:, h * HEAD : (h + 1) * HEAD] = acc[j * ROWS : (j + 1) * ROWS]
            logs = jnp.where(lane == h, log[j * ROWS : (j + 1) * ROWS], logs)
        high_ref[g], total_ref[g], sum_ref[g] = attend(queries(q_ref, g), g)
    for part in range(3):
        at = (20 + part) * HEAD
        piece = logs.astype(jnp.bfloat16)
        send_ref[:, at : at + HEAD] = piece
        logs = logs - piece.astype(jnp.float32)


def prefix_attend(q, q2, blocks, after):
    n = len(blocks)
    m = ROWS * GROUP
    keys = 2 * sum(b.shape[0] for b in blocks)
    return pl.pallas_call(
        functools.partial(prefix_kernel, n),
        out_shape=[
            jax.ShapeDtypeStruct((HEADS_KV, m, 1), jnp.float32),
            jax.ShapeDtypeStruct((HEADS_KV, m, 1), jnp.float32),
            jax.ShapeDtypeStruct((HEADS_KV, m, HEAD), jnp.float32),
            jax.ShapeDtypeStruct((ROWS, 23 * HEAD), jnp.bfloat16),
        ],
        in_specs=[VM] * (n + 2) + [ANY] * len(after),
        out_specs=[VM] * 4,
        compiler_params=PARAMS,
        cost_estimate=cost(4 * 1280 * keys * 128, keys * 2048 + 2000000, 1280 * keys),
    )(q, q2, *blocks, *after)


def last_kernel(
    where_ref, q_ref, t0, t1, t2, t3, own_ref, high_ref, total_ref, sum_ref, got_ref, out_ref
):
    x, parent = where_ref[2], where_ref[3]
    child = parent >= 0
    d = (parent - x) & 3
    row = lax.broadcasted_iota(jnp.int32, (ROWS, 2 * ROWS), 0)
    col = lax.broadcasted_iota(jnp.int32, (ROWS, 2 * ROWS), 1)
    use = (jnp.where(child, 1, 0) * jnp.where(col < ROWS, 1, 0)) + jnp.where(
        (col >= ROWS) & (col - ROWS <= row), 1, 0
    )
    use = jnp.concatenate([use] * GROUP, axis=0) > 0

    def pick(lo):
        a, b, c, e = (t[:, lo : lo + HEAD].astype(jnp.float32) for t in (t0, t1, t2, t3))
        return jnp.where(d == 0, a, jnp.where(d == 1, b, jnp.where(d == 2, c, e))).astype(
            jnp.bfloat16
        )

    logs = [got_ref[:, (20 + i) * HEAD : (21 + i) * HEAD].astype(jnp.float32) for i in range(3)]
    logs = logs[0] + logs[1] + logs[2]
    for g in range(HEADS_KV):
        q = queries(q_ref, g)
        lo, hi = g * HEAD, KEY_WIDTH + g * HEAD
        k = jnp.concatenate([pick(lo), own_ref[:, lo : lo + HEAD]], axis=0)
        v = jnp.concatenate([pick(hi), own_ref[:, hi : hi + HEAD]], axis=0)
        s = jnp.where(use, scores(q, k), NEG)
        heads = range(g * GROUP, (g + 1) * GROUP)
        high = high_ref[g]
        log = jnp.concatenate([logs[:, h : h + 1] for h in heads], axis=0)
        result = jnp.concatenate([got_ref[:, h * HEAD : (h + 1) * HEAD] for h in heads], axis=0)
        new = jnp.maximum(jnp.maximum(high, log), jnp.max(s, axis=-1, keepdims=True))
        p = jnp.exp2(s - new)
        factor, factor2 = jnp.exp2(high - new), jnp.exp2(log - new)
        total = total_ref[g] * factor + factor2 + jnp.sum(p, axis=-1, keepdims=True)
        acc = sum_ref[g] * factor + result.astype(jnp.float32) * factor2
        acc = acc + jnp.dot(p.astype(jnp.bfloat16), v, preferred_element_type=jnp.float32)
        acc = (acc / total).astype(jnp.bfloat16)
        for j in range(GROUP):
            lo = (g * GROUP + j) * HEAD
            out_ref[:, lo : lo + HEAD] = acc[j * ROWS : (j + 1) * ROWS]


def last_attend(where, q, trunks, own, state, got):
    return pl.pallas_call(
        last_kernel,
        out_shape=jax.ShapeDtypeStruct((ROWS, HEADS_KV * GROUP * HEAD), jnp.bfloat16),
        in_specs=[SM] + [VM] * 10,
        out_specs=VM,
        compiler_params=PARAMS,
        cost_estimate=cost(4 * 1280 * 128 * 128, 3000000, 1280 * 128),
    )(where, q, *trunks, own, *state, got)


def local(x_branch, w_kv, k_gain, q_branch, prefix_kv, tree_parent):
    y, core = lax.axis_index(Y), lax.axis_index("core")
    parent = tree_parent[0, 0]
    where = jnp.stack([core, y, lax.axis_index("x"), parent]).astype(jnp.int32)

    piece = prefix_kv[0]
    facing = along_y(piece, [(i, (i + 4) % 8) for i in range(8)])

    rows = x_branch[0]
    for_a, for_b = pack(rows, w_kv, facing)
    from_a = along_y(for_a, NEXT_A)
    from_b = along_y(for_b, NEXT_B)
    w_other = swap(w_kv)

    q = q_branch[0]
    q2 = ring_x(q, X_NEXT_A)

    piece = join([piece, facing])
    piece = join([piece, along_z(piece, 4)])
    piece = join([piece, along_z(piece, 2)])
    far = along_z(piece, 1)
    came_other = swap(weights(from_a, from_b, piece, q2))
    here, to_a, to_b = project(where, rows, w_kv, w_other, from_a, from_b, came_other)
    got_a = along_y(to_a, NEXT_A)
    got_b = along_y(to_b, NEXT_B)
    piece = join([piece, far], [to_a])
    beside = ring_x(piece, X_NEXT_B)

    index = jnp.arange(64, dtype=jnp.float32)
    inverse = jnp.exp(-jnp.log(jnp.float32(500000.0)) * 2.0 * index / HEAD)
    inside = jnp.arange(ROWS, dtype=jnp.int32)
    positions = PREFIX + inside + ROWS * (parent >= 0).astype(jnp.int32)
    angle = positions.astype(jnp.float32)[:, None] * inverse[None, :]
    cosine, sine = jnp.cos(angle), jnp.sin(angle)
    cosine = jnp.concatenate([cosine, cosine], axis=1)
    sine = jnp.concatenate([-sine, sine], axis=1)
    own = finish(where, here, got_a, got_b, k_gain[None, :], cosine, sine)

    root = (lax.axis_index("yh") == 0) & (lax.axis_index("z") == 0)
    have = jnp.where(root, own, jnp.zeros_like(own))
    for far in ((0, 4), (1, 0), (1, 4)):
        have = have + along_yh_z(own, [(0, 0) + far])
    trunk = have
    for step in (1, -1, 2):
        trunk = trunk + along_yh_z(
            have, [(a, b, a, (b + step) % 8) for a in range(2) for b in (0, 4)]
        )
    *state, partial = prefix_attend(q, q2, [piece, beside], [have])
    trunks = [trunk, along_x(trunk, -1), along_x(trunk, 2), along_x(trunk, 1)]
    return last_attend(where, q, trunks, own, state, ring_x(partial, X_NEXT_A))[None]


def solution(mesh):
    parts = jax.sharding.Mesh(mesh.devices.reshape(SIZES), PARTS)
    tokens = P(NARROW, WIDE, None)
    placed = (tokens, P(None, NARROW), P(), tokens, tokens, P(NARROW, WIDE))
    return jax.shard_map(local, mesh=parts, in_specs=placed, out_specs=tokens, check_vma=False)
```

time: 137 us -> 116 us (0.85)
  the two profiles are of different devices: /device:TPU:48 before, /device:TPU:8 now
where the time goes in v2:
time: 116 us
  starting transfers between devices  77.5 us (67%)
  waiting for transfers between devices  23.1 us (20%)
  Pallas kernels  12.4 us (11%)
    ppermute x5, starting transfers between devices, along_y(): return lax.ppermute(value, Y, pairs)  24 us
    ppermute x3, starting transfers between devices, along_z(): return lax.ppermute(value, 'z', [(i, i ^ bit) for i in range(8)])  17.4 us
    ppermute x6, starting transfers between devices, along_yh_z(): lax.ppermute(value, ('yh', 'z'), [(a * 8 + b, c * 8 + d) for a, b, c, d i...  14.7 us
    ppermute x3, starting transfers between devices, along_x(): return lax.ppermute(value, 'x', [(i, (i + s) % 4) for i in range(4)])  9.23 us
    ppermute x6, waiting for transfers between devices, along_yh_z(): lax.ppermute(value, ('yh', 'z'), [(a * 8 + b, c * 8 + d) for a, b, c, d i...  8.91 us
    ppermute x3, starting transfers between devices, ring_x(): return lax.ppermute(value, 'x', pairs)  8.43 us
    ppermute x3, waiting for transfers between devices, along_x(): return lax.ppermute(value, 'x', [(i, (i + s) % 4) for i in range(4)])  6.14 us
    ppermute x3, waiting for transfers between devices, along_z(): return lax.ppermute(value, 'z', [(i, i ^ bit) for i in range(8)])  4.85 us
  transfers between devices with their start and end apart: 22, of which 8 were waited for; matrix products, arithmetic and copies ran while one was open for 0% of the time, Pallas kernels for 6%

profile of v2, /device:TPU:8, one launch (start us, length us, event | category | flops | bytes accessed | tf_op | source)
XLA Modules:
  0.0 115.7 jit_solution(6034790196681426178)
XLA Ops:
  0.0 6.8 %collective-permute-start.1 = (bf16[16,1024]{1,0:T(8,128)(2,1)}, bf16[16,1024]{1,0:T(8,128)(2,1)S(1)}, u32[]{:S(2)}, u32[]{:S(2)}) collective-permute-start(bf16[16,1024]{1,0:T(8,128)(2,1)} %bitcast.16), channel_id=1, source_target_pairs={{0,256},{2,258},{4,260},{6,262},{256,0},{258,2},{260,4},{262,6},{1... | collective-permute-start | bytes 98312 | tf_op jit(solution)/shard_map/ppermute | solution.py:43
  6.8 3.2 %collective-permute-done.1.after_ref.refs_1_ = bf16[16,1024]{1,0:T(8,128)(2,1)S(1)} collective-permute-done((bf16[16,1024]{1,0:T(8,128)(2,1)}, bf16[16,1024]{1,0:T(8,128)(2,1)S(1)}, u32[]{:S(2)}, u32[]{:S(2)}) %collective-permute-start.1) | collective-permute-done | bytes 32800 | tf_op jit(solution)/shard_map/ppermute | solution.py:43
  12.7 7.6 %collective-permute-start.2 = (bf16[3840,128]{1,0:T(8,128)(2,1)S(1)}, bf16[3840,128]{1,0:T(8,128)(2,1)S(1)}, u32[]{:S(2)}, u32[]{:S(2)}) collective-permute-start(bf16[3840,128]{1,0:T(8,128)(2,1)S(1)} %get-tuple-element.14), channel_id=1, source_target_pairs={{0,2},{2,0},{4,6},{6,4},{256,258},{258,256},{260,262},{262,260},{1... | collective-permute-start | bytes 2949128 | tf_op jit(solution)/shard_map/ppermute | solution.py:43
  20.3 1.9 %collective-permute-start.3 = (bf16[3840,128]{1,0:T(8,128)(2,1)S(1)}, bf16[3840,128]{1,0:T(8,128)(2,1)S(1)}, u32[]{:S(2)}, u32[]{:S(2)}) collective-permute-start(bf16[3840,128]{1,0:T(8,128)(2,1)S(1)} %get-tuple-element.15), channel_id=1, source_target_pairs={{0,262},{2,4},{4,2},{6,256},{256,6},{258,260},{260,258},{262,0},{1... | collective-permute-start | bytes 2949128 | tf_op jit(solution)/shard_map/ppermute | solution.py:43
  22.2 1.9 %collective-permute-start.6 = (bf16[64,2560]{1,0:T(8,128)(2,1)S(1)}, bf16[64,2560]{1,0:T(8,128)(2,1)S(1)}, u32[]{:S(2)}, u32[]{:S(2)}) collective-permute-start(bf16[64,2560]{1,0:T(8,128)(2,1)S(1)} %bitcast.13), channel_id=1, source_target_pairs={{0,8},{8,0},{16,24},{24,16},{1,9},{9,1},{17,25},{25,17},{2,10},{10... | collective-permute-start | bytes 983048 | tf_op jit(solution)/shard_map/ppermute | solution.py:35
  24.2 9.7 %collective-permute-start.4 = (bf16[32,1024]{1,0:T(8,128)(2,1)S(1)}, bf16[32,1024]{1,0:T(8,128)(2,1)S(1)}, u32[]{:S(2)}, u32[]{:S(2)}) collective-permute-start(bf16[32,1024]{1,0:T(8,128)(2,1)S(1)} %shard_map.65.refs_0_), channel_id=1, source_target_pairs={{0,128},{32,160},{64,192},{96,224},{128,0},{160,32},{192,64},{224,... | collective-permute-start | bytes 196616 | tf_op jit(solution)/shard_map/ppermute | solution.py:47
  33.9 2.4 %collective-permute-done.4.refs_1_ = bf16[32,1024]{1,0:T(8,128)(2,1)S(1)} collective-permute-done((bf16[32,1024]{1,0:T(8,128)(2,1)S(1)}, bf16[32,1024]{1,0:T(8,128)(2,1)S(1)}, u32[]{:S(2)}, u32[]{:S(2)}) %collective-permute-start.4) | collective-permute-done | bytes 65568 | tf_op jit(solution)/shard_map/ppermute | solution.py:47
  36.4 4.9 %collective-permute-start.5 = (bf16[64,1024]{1,0:T(8,128)(2,1)S(1)}, bf16[64,1024]{1,0:T(8,128)(2,1)S(1)}, u32[]{:S(2)}, u32[]{:S(2)}) collective-permute-start(bf16[64,1024]{1,0:T(8,128)(2,1)S(1)} %shard_map.66.refs_0_), channel_id=1, source_target_pairs={{0,64},{32,96},{64,0},{96,32},{128,192},{160,224},{192,128},{224,1... | collective-permute-start | bytes 393224 | tf_op jit(solution)/shard_map/ppermute | solution.py:47
  41.2 1.9 %collective-permute-start = (bf16[5120,128]{1,0:T(8,128)(2,1)}, bf16[5120,128]{1,0:T(8,128)(2,1)}, u32[]{:S(2)}, u32[]{:S(2)}) collective-permute-start(bf16[5120,128]{1,0:T(8,128)(2,1)} %own.1), channel_id=1, source_target_pairs={{0,1},{1,0},{2,3},{3,2},{4,5},{5,4},{6,7},{7,6},{8,9},{9,8},{10,11... | collective-permute-start | bytes 3932168 | tf_op jit(solution)/shard_map/ppermute | solution.py:51
  43.2 2.4 %collective-permute-done.5.refs_1_ = bf16[64,1024]{1,0:T(8,128)(2,1)S(1)} collective-permute-done((bf16[64,1024]{1,0:T(8,128)(2,1)S(1)}, bf16[64,1024]{1,0:T(8,128)(2,1)S(1)}, u32[]{:S(2)}, u32[]{:S(2)}) %collective-permute-start.5) | collective-permute-done | bytes 131104 | tf_op jit(solution)/shard_map/ppermute | solution.py:47
  49.5 2.8 %collective-permute-start.19 = (bf16[128,1024]{1,0:T(8,128)(2,1)S(1)}, bf16[128,1024]{1,0:T(8,128)(2,1)S(1)}, u32[]{:S(2)}, u32[]{:S(2)}) collective-permute-start(bf16[128,1024]{1,0:T(8,128)(2,1)S(1)} %shard_map.67.piece_ref.refs_0_), channel_id=1, source_target_pairs={{0,32},{32,0},{64,96},{96,64},{128,160},{160,128},{192,224},{224,1... | collective-permute-start | bytes 786440 | tf_op jit(solution)/shard_map/ppermute | solution.py:47
  52.6 3.0 %shard_map.69 = (f32[64,768]{1,0:T(8,128)S(1)}, bf16[64,512]{1,0:T(8,128)(2,1)S(1)}, bf16[64,512]{1,0:T(8,128)(2,1)S(1)}) custom-call(s32[4]{0:T(128)S(1)} %pad_add_fusion.where_ref, bf16[64,5120]{1,0:T(8,128)(2,1)S(1)} %bitcast.12, bf16[5120,128]{1,0:T(8,128)(2,1)} %own.1, bf16[5120,128]{1,0:T(8,128)(2,1)} %collective-permute-done.other, ...), custom_call_target="tpu_custom_call" | custom-call | flops 671088640 | bytes 7000000 | tf_op jit(solution)/shard_map/pallas_call | solution.py:175
  55.6 4.0 %collective-permute-start.8 = (bf16[64,512]{1,0:T(8,128)(2,1)S(1)}, bf16[64,512]{1,0:T(8,128)(2,1)S(1)}, u32[]{:S(2)}, u32[]{:S(2)}) collective-permute-start(bf16[64,512]{1,0:T(8,128)(2,1)S(1)} %get-tuple-element.17.refs_2_), channel_id=1, source_target_pairs={{0,2},{2,0},{4,6},{6,4},{256,258},{258,256},{260,262},{262,260},{1... | collective-permute-start | bytes 196616 | tf_op jit(solution)/shard_map/ppermute | solution.py:43
  59.6 3.6 %collective-permute-start.9 = (bf16[64,512]{1,0:T(8,128)(2,1)S(1)}, bf16[64,512]{1,0:T(8,128)(2,1)S(1)}, u32[]{:S(2)}, u32[]{:S(2)}) collective-permute-start(bf16[64,512]{1,0:T(8,128)(2,1)S(1)} %get-tuple-element.18), channel_id=1, source_target_pairs={{0,262},{2,4},{4,2},{6,256},{256,6},{258,260},{260,258},{262,0},{1... | collective-permute-start | bytes 196616 | tf_op jit(solution)/shard_map/ppermute | solution.py:43
  63.3 4.0 %collective-permute-start.20 = (bf16[256,1024]{1,0:T(8,128)(2,1)S(1)}, bf16[256,1024]{1,0:T(8,128)(2,1)S(1)}, u32[]{:S(2)}, u32[]{:S(2)}) collective-permute-start(bf16[256,1024]{1,0:T(8,128)(2,1)S(1)} %shard_map.71.refs_0_), channel_id=1, source_target_pairs={{0,24},{8,16},{16,8},{24,0},{1,25},{9,17},{17,9},{25,1},{2,26},{10... | collective-permute-start | bytes 1572872 | tf_op jit(solution)/shard_map/ppermute | solution.py:35
  68.2 7.8 %collective-permute-start.10 = (bf16[64,1024]{1,0:T(8,128)(2,1)S(1)}, bf16[64,1024]{1,0:T(8,128)(2,1)S(1)}, u32[]{:S(2)}, u32[]{:S(2)}) collective-permute-start(bf16[64,1024]{1,0:T(8,128)(2,1)S(1)} %shard_map.70.own_ref), channel_id=1, source_target_pairs={{0,128},{1,129},{2,130},{3,131},{4,132},{5,133},{6,134},{7,135},{8... | collective-permute-start | bytes 393224 | tf_op jit(solution)/shard_map/ppermute | solution.py:55
  79.0 7.0 %collective-permute-done.11 = bf16[64,1024]{1,0:T(8,128)(2,1)S(1)} collective-permute-done((bf16[64,1024]{1,0:T(8,128)(2,1)S(1)}, bf16[64,1024]{1,0:T(8,128)(2,1)S(1)}, u32[]{:S(2)}, u32[]{:S(2)}) %collective-permute-start.11) | collective-permute-done | bytes 131104 | tf_op jit(solution)/shard_map/ppermute | solution.py:55
  91.9 2.1 %shard_map.72 = (f32[4,320,1]{2,1,0:T(8,128)S(1)}, f32[4,320,1]{2,1,0:T(8,128)S(1)}, f32[4,320,128]{2,1,0:T(8,128)S(1)}, bf16[64,2944]{1,0:T(8,128)(2,1)S(1)}) custom-call(bf16[64,2560]{1,0:T(8,128)(2,1)S(1)} %bitcast.14, bf16[64,2560]{1,0:T(8,128)(2,1)S(1)} %collective-permute-done.6.q_ref.q2_ref, bf16[256,1024]{1,0:T(8,128)(2,1)S(1)} %shard_map.71.refs_0_, ...), custom_call_target="tpu_custom_call" | custom-call | flops 671088640 | bytes 4097152 | tf_op jit(solution)/shard_map/pallas_call | solution.py:276
  94.0 2.5 %collective-permute-start.21 = (bf16[64,2944]{1,0:T(8,128)(2,1)S(1)}, bf16[64,2944]{1,0:T(8,128)(2,1)S(1)}, u32[]{:S(2)}, u32[]{:S(2)}) collective-permute-start(bf16[64,2944]{1,0:T(8,128)(2,1)S(1)} %get-tuple-element.22), channel_id=1, source_target_pairs={{0,8},{8,0},{16,24},{24,16},{1,9},{9,1},{17,25},{25,17},{2,10},{10... | collective-permute-start | bytes 1130504 | tf_op jit(solution)/shard_map/ppermute | solution.py:35
  96.6 3.0 %collective-permute-start.16 = (bf16[64,1024]{1,0:T(8,128)(2,1)S(1)}, bf16[64,1024]{1,0:T(8,128)(2,1)S(1)}, u32[]{:S(2)}, u32[]{:S(2)}) collective-permute-start(bf16[64,1024]{1,0:T(8,128)(2,1)S(1)} %add_add_fusion.t0), channel_id=1, source_target_pairs={{0,24},{8,0},{16,8},{24,16},{1,25},{9,1},{17,9},{25,17},{2,26},{10... | collective-permute-start | bytes 393224 | tf_op jit(solution)/shard_map/ppermute | solution.py:39
  99.6 4.3 %collective-permute-start.17 = (bf16[64,1024]{1,0:T(8,128)(2,1)S(1)}, bf16[64,1024]{1,0:T(8,128)(2,1)S(1)}, u32[]{:S(2)}, u32[]{:S(2)}) collective-permute-start(bf16[64,1024]{1,0:T(8,128)(2,1)S(1)} %add_add_fusion.t0), channel_id=1, source_target_pairs={{0,16},{8,24},{16,0},{24,8},{1,17},{9,25},{17,1},{25,9},{2,18},{10... | collective-permute-start | bytes 393224 | tf_op jit(solution)/shard_map/ppermute | solution.py:39
  103.9 1.9 %collective-permute-start.18 = (bf16[64,1024]{1,0:T(8,128)(2,1)S(1)}, bf16[64,1024]{1,0:T(8,128)(2,1)S(1)}, u32[]{:S(2)}, u32[]{:S(2)}) collective-permute-start(bf16[64,1024]{1,0:T(8,128)(2,1)S(1)} %add_add_fusion.t0), channel_id=1, source_target_pairs={{0,8},{8,16},{16,24},{24,0},{1,9},{9,17},{17,25},{25,1},{2,10},{10... | collective-permute-start | bytes 393224 | tf_op jit(solution)/shard_map/ppermute | solution.py:39
  105.8 4.1 %collective-permute-done.16.t1 = bf16[64,1024]{1,0:T(8,128)(2,1)S(1)} collective-permute-done((bf16[64,1024]{1,0:T(8,128)(2,1)S(1)}, bf16[64,1024]{1,0:T(8,128)(2,1)S(1)}, u32[]{:S(2)}, u32[]{:S(2)}) %collective-permute-start.16) | collective-permute-done | bytes 131104 | tf_op jit(solution)/shard_map/ppermute | solution.py:39
  112.0 3.7 %shard_map.73 = bf16[64,2560]{1,0:T(8,128)(2,1)} custom-call(s32[4]{0:T(128)S(1)} %pad_add_fusion.where_ref, bf16[64,2560]{1,0:T(8,128)(2,1)S(1)} %bitcast.15, bf16[64,1024]{1,0:T(8,128)(2,1)S(1)} %add_add_fusion.t0, bf16[64,1024]{1,0:T(8,128)(2,1)S(1)} %collective-permute-done.16.t1, bf16[64,1024]{1,0:T(8,128)(2,1)S(1)} %collective-permute-done.17.t2, ...), custom_call_target="tpu_custom_call" | custom-call | flops 83886080 | bytes 3000000 | tf_op jit(solution)/shard_map/pallas_call | solution.py:335
  (47 shorter events, 17.9 us)
Async XLA Ops:
  0.0 10.0 %collective-permute-start.1 = (bf16[16,1024]{1,0:T(8,128)(2,1)}, bf16[16,1024]{1,0:T(8,128)(2,1)S(1)}, u32[]{:S(2)}, u32[]{:S(2)}) collective-permute-start(bf16[16,1024]{1,0:T(8,128)(2,1)} %bitcast.16), channel_id=1, source_target_pairs={{0,256},{2,258},{4,260},{6,262},{256,0},{258,2},{260,4},{262,6},{1... | collective-permute-start | bytes 98312 | tf_op jit(solution)/shard_map/ppermute | solution.py:43
  11.1 13.1 %copy-start.3 = (bf16[1,16,1024]{2,1,0:T(8,128)(2,1)S(1)}, bf16[1,16,1024]{2,1,0:T(8,128)(2,1)}, u32[]{:S(2)}) copy-start(bf16[1,16,1024]{2,1,0:T(8,128)(2,1)} %param.10) | copy-start | bytes 98308
  12.7 33.0 %collective-permute-start.2 = (bf16[3840,128]{1,0:T(8,128)(2,1)S(1)}, bf16[3840,128]{1,0:T(8,128)(2,1)S(1)}, u32[]{:S(2)}, u32[]{:S(2)}) collective-permute-start(bf16[3840,128]{1,0:T(8,128)(2,1)S(1)} %get-tuple-element.14), channel_id=1, source_target_pairs={{0,2},{2,0},{4,6},{6,4},{256,258},{258,256},{260,262},{262,260},{1... | collective-permute-start | bytes 2949128 | tf_op jit(solution)/shard_map/ppermute | solution.py:43
  20.3 25.3 %collective-permute-start.3 = (bf16[3840,128]{1,0:T(8,128)(2,1)S(1)}, bf16[3840,128]{1,0:T(8,128)(2,1)S(1)}, u32[]{:S(2)}, u32[]{:S(2)}) collective-permute-start(bf16[3840,128]{1,0:T(8,128)(2,1)S(1)} %get-tuple-element.15), channel_id=1, source_target_pairs={{0,262},{2,4},{4,2},{6,256},{256,6},{258,260},{260,258},{262,0},{1... | collective-permute-start | bytes 2949128 | tf_op jit(solution)/shard_map/ppermute | solution.py:43
  22.2 23.4 %collective-permute-start.6 = (bf16[64,2560]{1,0:T(8,128)(2,1)S(1)}, bf16[64,2560]{1,0:T(8,128)(2,1)S(1)}, u32[]{:S(2)}, u32[]{:S(2)}) collective-permute-start(bf16[64,2560]{1,0:T(8,128)(2,1)S(1)} %bitcast.13), channel_id=1, source_target_pairs={{0,8},{8,0},{16,24},{24,16},{1,9},{9,1},{17,25},{25,17},{2,10},{10... | collective-permute-start | bytes 983048 | tf_op jit(solution)/shard_map/ppermute | solution.py:35
  24.2 12.2 %collective-permute-start.4 = (bf16[32,1024]{1,0:T(8,128)(2,1)S(1)}, bf16[32,1024]{1,0:T(8,128)(2,1)S(1)}, u32[]{:S(2)}, u32[]{:S(2)}) collective-permute-start(bf16[32,1024]{1,0:T(8,128)(2,1)S(1)} %shard_map.65.refs_0_), channel_id=1, source_target_pairs={{0,128},{32,160},{64,192},{96,224},{128,0},{160,32},{192,64},{224,... | collective-permute-start | bytes 196616 | tf_op jit(solution)/shard_map/ppermute | solution.py:47
  36.4 9.2 %collective-permute-start.5 = (bf16[64,1024]{1,0:T(8,128)(2,1)S(1)}, bf16[64,1024]{1,0:T(8,128)(2,1)S(1)}, u32[]{:S(2)}, u32[]{:S(2)}) collective-permute-start(bf16[64,1024]{1,0:T(8,128)(2,1)S(1)} %shard_map.66.refs_0_), channel_id=1, source_target_pairs={{0,64},{32,96},{64,0},{96,32},{128,192},{160,224},{192,128},{224,1... | collective-permute-start | bytes 393224 | tf_op jit(solution)/shard_map/ppermute | solution.py:47
  41.2 11.3 %collective-permute-start = (bf16[5120,128]{1,0:T(8,128)(2,1)}, bf16[5120,128]{1,0:T(8,128)(2,1)}, u32[]{:S(2)}, u32[]{:S(2)}) collective-permute-start(bf16[5120,128]{1,0:T(8,128)(2,1)} %own.1), channel_id=1, source_target_pairs={{0,1},{1,0},{2,3},{3,2},{4,5},{5,4},{6,7},{7,6},{8,9},{9,8},{10,11... | collective-permute-start | bytes 3932168 | tf_op jit(solution)/shard_map/ppermute | solution.py:51
  46.8 5.8 %collective-permute-start.7 = (bf16[5120,128]{1,0:T(8,128)(2,1)}, bf16[5120,128]{1,0:T(8,128)(2,1)}, u32[]{:S(2)}, u32[]{:S(2)}) collective-permute-start(bf16[5120,128]{1,0:T(8,128)(2,1)} %shard_map.68), channel_id=1, source_target_pairs={{0,1},{1,0},{2,3},{3,2},{4,5},{5,4},{6,7},{7,6},{8,9},{9,8},{10,11... | collective-permute-start | bytes 3932168 | tf_op jit(solution)/shard_map/ppermute | solution.py:51
  49.5 13.7 %collective-permute-start.19 = (bf16[128,1024]{1,0:T(8,128)(2,1)S(1)}, bf16[128,1024]{1,0:T(8,128)(2,1)S(1)}, u32[]{:S(2)}, u32[]{:S(2)}) collective-permute-start(bf16[128,1024]{1,0:T(8,128)(2,1)S(1)} %shard_map.67.piece_ref.refs_0_), channel_id=1, source_target_pairs={{0,32},{32,0},{64,96},{96,64},{128,160},{160,128},{192,224},{224,1... | collective-permute-start | bytes 786440 | tf_op jit(solution)/shard_map/ppermute | solution.py:47
  52.5 14.8 %copy-start.4 = (f32[512]{0:T(512)S(1)}, f32[512]{0:T(512)}, u32[]{:S(2)}) copy-start(f32[512]{0:T(512)} %param.8) | copy-start | bytes 6148
  55.6 11.8 %collective-permute-start.8 = (bf16[64,512]{1,0:T(8,128)(2,1)S(1)}, bf16[64,512]{1,0:T(8,128)(2,1)S(1)}, u32[]{:S(2)}, u32[]{:S(2)}) collective-permute-start(bf16[64,512]{1,0:T(8,128)(2,1)S(1)} %get-tuple-element.17.refs_2_), channel_id=1, source_target_pairs={{0,2},{2,0},{4,6},{6,4},{256,258},{258,256},{260,262},{262,260},{1... | collective-permute-start | bytes 196616 | tf_op jit(solution)/shard_map/ppermute | solution.py:43
  59.6 7.8 %collective-permute-start.9 = (bf16[64,512]{1,0:T(8,128)(2,1)S(1)}, bf16[64,512]{1,0:T(8,128)(2,1)S(1)}, u32[]{:S(2)}, u32[]{:S(2)}) collective-permute-start(bf16[64,512]{1,0:T(8,128)(2,1)S(1)} %get-tuple-element.18), channel_id=1, source_target_pairs={{0,262},{2,4},{4,2},{6,256},{256,6},{258,260},{260,258},{262,0},{1... | collective-permute-start | bytes 196616 | tf_op jit(solution)/shard_map/ppermute | solution.py:43
  63.3 28.6 %collective-permute-start.20 = (bf16[256,1024]{1,0:T(8,128)(2,1)S(1)}, bf16[256,1024]{1,0:T(8,128)(2,1)S(1)}, u32[]{:S(2)}, u32[]{:S(2)}) collective-permute-start(bf16[256,1024]{1,0:T(8,128)(2,1)S(1)} %shard_map.71.refs_0_), channel_id=1, source_target_pairs={{0,24},{8,16},{16,8},{24,0},{1,25},{9,17},{17,9},{25,1},{2,26},{10... | collective-permute-start | bytes 1572872 | tf_op jit(solution)/shard_map/ppermute | solution.py:35
  68.2 10.8 %collective-permute-start.10 = (bf16[64,1024]{1,0:T(8,128)(2,1)S(1)}, bf16[64,1024]{1,0:T(8,128)(2,1)S(1)}, u32[]{:S(2)}, u32[]{:S(2)}) collective-permute-start(bf16[64,1024]{1,0:T(8,128)(2,1)S(1)} %shard_map.70.own_ref), channel_id=1, source_target_pairs={{0,128},{1,129},{2,130},{3,131},{4,132},{5,133},{6,134},{7,135},{8... | collective-permute-start | bytes 393224 | tf_op jit(solution)/shard_map/ppermute | solution.py:55
  76.0 10.0 %collective-permute-start.11 = (bf16[64,1024]{1,0:T(8,128)(2,1)S(1)}, bf16[64,1024]{1,0:T(8,128)(2,1)S(1)}, u32[]{:S(2)}, u32[]{:S(2)}) collective-permute-start(bf16[64,1024]{1,0:T(8,128)(2,1)S(1)} %shard_map.70.own_ref), channel_id=1, source_target_pairs={{0,256},{1,257},{2,258},{3,259},{4,260},{5,261},{6,262},{7,263},{8... | collective-permute-start | bytes 393224 | tf_op jit(solution)/shard_map/ppermute | solution.py:55
  77.3 10.6 %collective-permute-start.12 = (bf16[64,1024]{1,0:T(8,128)(2,1)S(1)}, bf16[64,1024]{1,0:T(8,128)(2,1)S(1)}, u32[]{:S(2)}, u32[]{:S(2)}) collective-permute-start(bf16[64,1024]{1,0:T(8,128)(2,1)S(1)} %shard_map.70.own_ref), channel_id=1, source_target_pairs={{0,384},{1,385},{2,386},{3,387},{4,388},{5,389},{6,390},{7,391},{8... | collective-permute-start | bytes 393224 | tf_op jit(solution)/shard_map/ppermute | solution.py:55
  87.9 8.6 %collective-permute-start.13 = (bf16[64,1024]{1,0:T(8,128)(2,1)S(1)}, bf16[64,1024]{1,0:T(8,128)(2,1)S(1)}, u32[]{:S(2)}, u32[]{:S(2)}) collective-permute-start(bf16[64,1024]{1,0:T(8,128)(2,1)S(1)} %add_add_fusion.1.refs_2_), channel_id=1, source_target_pairs={{0,32},{128,160},{256,288},{384,416},{1,33},{129,161},{257,289},{3... | collective-permute-start | bytes 393224 | tf_op jit(solution)/shard_map/ppermute | solution.py:55
  89.2 7.3 %collective-permute-start.14 = (bf16[64,1024]{1,0:T(8,128)(2,1)S(1)}, bf16[64,1024]{1,0:T(8,128)(2,1)S(1)}, u32[]{:S(2)}, u32[]{:S(2)}) collective-permute-start(bf16[64,1024]{1,0:T(8,128)(2,1)S(1)} %add_add_fusion.1.refs_2_), channel_id=1, source_target_pairs={{0,224},{128,96},{256,480},{384,352},{1,225},{129,97},{257,481},{3... | collective-permute-start | bytes 393224 | tf_op jit(solution)/shard_map/ppermute | solution.py:55
  90.5 6.0 %collective-permute-start.15 = (bf16[64,1024]{1,0:T(8,128)(2,1)S(1)}, bf16[64,1024]{1,0:T(8,128)(2,1)S(1)}, u32[]{:S(2)}, u32[]{:S(2)}) collective-permute-start(bf16[64,1024]{1,0:T(8,128)(2,1)S(1)} %add_add_fusion.1.refs_2_), channel_id=1, source_target_pairs={{0,64},{128,192},{256,320},{384,448},{1,65},{129,193},{257,321},{3... | collective-permute-start | bytes 393224 | tf_op jit(solution)/shard_map/ppermute | solution.py:55
  94.0 18.0 %collective-permute-start.21 = (bf16[64,2944]{1,0:T(8,128)(2,1)S(1)}, bf16[64,2944]{1,0:T(8,128)(2,1)S(1)}, u32[]{:S(2)}, u32[]{:S(2)}) collective-permute-start(bf16[64,2944]{1,0:T(8,128)(2,1)S(1)} %get-tuple-element.22), channel_id=1, source_target_pairs={{0,8},{8,0},{16,24},{24,16},{1,9},{9,1},{17,25},{25,17},{2,10},{10... | collective-permute-start | bytes 1130504 | tf_op jit(solution)/shard_map/ppermute | solution.py:35
  96.6 13.4 %collective-permute-start.16 = (bf16[64,1024]{1,0:T(8,128)(2,1)S(1)}, bf16[64,1024]{1,0:T(8,128)(2,1)S(1)}, u32[]{:S(2)}, u32[]{:S(2)}) collective-permute-start(bf16[64,1024]{1,0:T(8,128)(2,1)S(1)} %add_add_fusion.t0), channel_id=1, source_target_pairs={{0,24},{8,0},{16,8},{24,16},{1,25},{9,1},{17,9},{25,17},{2,26},{10... | collective-permute-start | bytes 393224 | tf_op jit(solution)/shard_map/ppermute | solution.py:39
  99.6 10.7 %collective-permute-start.17 = (bf16[64,1024]{1,0:T(8,128)(2,1)S(1)}, bf16[64,1024]{1,0:T(8,128)(2,1)S(1)}, u32[]{:S(2)}, u32[]{:S(2)}) collective-permute-start(bf16[64,1024]{1,0:T(8,128)(2,1)S(1)} %add_add_fusion.t0), channel_id=1, source_target_pairs={{0,16},{8,24},{16,0},{24,8},{1,17},{9,25},{17,1},{25,9},{2,18},{10... | collective-permute-start | bytes 393224 | tf_op jit(solution)/shard_map/ppermute | solution.py:39
  103.9 8.1 %collective-permute-start.18 = (bf16[64,1024]{1,0:T(8,128)(2,1)S(1)}, bf16[64,1024]{1,0:T(8,128)(2,1)S(1)}, u32[]{:S(2)}, u32[]{:S(2)}) collective-permute-start(bf16[64,1024]{1,0:T(8,128)(2,1)S(1)} %add_add_fusion.t0), channel_id=1, source_target_pairs={{0,8},{8,16},{16,24},{24,0},{1,9},{9,17},{17,25},{25,1},{2,10},{10... | collective-permute-start | bytes 393224 | tf_op jit(solution)/shard_map/ppermute | solution.py:39
  (3 other events, 19.2 us)

commit v3 on v2

--- a/solution.py
+++ b/solution.py
@@ -57,7 +57,7 @@
 
 VM = pl.BlockSpec(memory_space=pltpu.VMEM)
 SM = pl.BlockSpec(memory_space=pltpu.SMEM)
-PARAMS = pltpu.CompilerParams(vmem_limit_bytes=40 * 1024 * 1024)
+PARAMS = pltpu.CompilerParams(vmem_limit_bytes=20 * 1024 * 1024)
 
 
 def cost(flops, moved, trans=0):
@@ -230,6 +230,23 @@
     ) * SCALE
 
 
+def merge_kernel(*refs):
+    parts, out_ref = refs[:4], refs[-1]
+    a, b, c, d = (p[...].astype(jnp.float32) for p in parts)
+    out_ref[...] = (a + b + c + d).astype(jnp.bfloat16)
+
+
+def merge(parts):
+    return pl.pallas_call(
+        merge_kernel,
+        out_shape=jax.ShapeDtypeStruct(parts[0].shape, parts[0].dtype),
+        in_specs=[VM] * 4,
+        out_specs=VM,
+        compiler_params=PARAMS,
+        cost_estimate=cost(0, 10 * parts[0].size),
+    )(*parts)
+
+
 def prefix_kernel(n, q_ref, q2_ref, *refs):
     blocks, (high_ref, total_ref, sum_ref, send_ref) = refs[:n], refs[-4:]
     lane = lax.broadcasted_iota(jnp.int32, (ROWS, HEAD), 1)
@@ -255,7 +272,7 @@
 
     for g in range(HEADS_KV):
         high, total, acc = attend(queries(q2_ref, g), g)
-        acc = (acc / total).astype(jnp.bfloat16)
+        acc = (acc * (1.0 / total)).astype(jnp.bfloat16)
         log = high + jnp.log2(total)
         for j in range(GROUP):
             h = g * GROUP + j
@@ -289,7 +306,7 @@
 
 
 def last_kernel(
-    where_ref, q_ref, t0, t1, t2, t3, own_ref, high_ref, total_ref, sum_ref, got_ref, out_ref
+    where_ref, q_ref, t0, t1, t2, t3, own_ref, high_ref, total_ref, sum_ref, got_ref, out_ref, above_ref
 ):
     x, parent = where_ref[2], where_ref[3]
     child = parent >= 0
@@ -301,19 +318,19 @@
     )
     use = jnp.concatenate([use] * GROUP, axis=0) > 0
 
-    def pick(lo):
-        a, b, c, e = (t[:, lo : lo + HEAD].astype(jnp.float32) for t in (t0, t1, t2, t3))
-        return jnp.where(d == 0, a, jnp.where(d == 1, b, jnp.where(d == 2, c, e))).astype(
-            jnp.bfloat16
-        )
+    for k, t in enumerate((t0, t1, t2, t3)):
+
+        @pl.when(d == k)
+        def _(t=t):
+            above_ref[...] = t[...]
 
     logs = [got_ref[:, (20 + i) * HEAD : (21 + i) * HEAD].astype(jnp.float32) for i in range(3)]
     logs = logs[0] + logs[1] + logs[2]
     for g in range(HEADS_KV):
         q = queries(q_ref, g)
         lo, hi = g * HEAD, KEY_WIDTH + g * HEAD
-        k = jnp.concatenate([pick(lo), own_ref[:, lo : lo + HEAD]], axis=0)
-        v = jnp.concatenate([pick(hi), own_ref[:, hi : hi + HEAD]], axis=0)
+        k = jnp.concatenate([above_ref[:, lo : lo + HEAD], own_ref[:, lo : lo + HEAD]], axis=0)
+        v = jnp.concatenate([above_ref[:, hi : hi + HEAD], own_ref[:, hi : hi + HEAD]], axis=0)
         s = jnp.where(use, scores(q, k), NEG)
         heads = range(g * GROUP, (g + 1) * GROUP)
         high = high_ref[g]
@@ -325,7 +342,7 @@
         total = total_ref[g] * factor + factor2 + jnp.sum(p, axis=-1, keepdims=True)
         acc = sum_ref[g] * factor + result.astype(jnp.float32) * factor2
         acc = acc + jnp.dot(p.astype(jnp.bfloat16), v, preferred_element_type=jnp.float32)
-        acc = (acc / total).astype(jnp.bfloat16)
+        acc = (acc * (1.0 / total)).astype(jnp.bfloat16)
         for j in range(GROUP):
             lo = (g * GROUP + j) * HEAD
             out_ref[:, lo : lo + HEAD] = acc[j * ROWS : (j + 1) * ROWS]
@@ -337,6 +354,7 @@
         out_shape=jax.ShapeDtypeStruct((ROWS, HEADS_KV * GROUP * HEAD), jnp.bfloat16),
         in_specs=[SM] + [VM] * 10,
         out_specs=VM,
+        scratch_shapes=[pltpu.VMEM((ROWS, 2 * KEY_WIDTH), jnp.bfloat16)],
         compiler_params=PARAMS,
         cost_estimate=cost(4 * 1280 * 128 * 128, 3000000, 1280 * 128),
     )(where, q, *trunks, own, *state, got)
@@ -360,14 +378,14 @@
     q2 = ring_x(q, X_NEXT_A)
 
     piece = join([piece, facing])
-    piece = join([piece, along_z(piece, 4)])
-    piece = join([piece, along_z(piece, 2)])
+    for bit in (4, 2):
+        piece = join([piece, along_z(piece, bit)])
     far = along_z(piece, 1)
     came_other = swap(weights(from_a, from_b, piece, q2))
     here, to_a, to_b = project(where, rows, w_kv, w_other, from_a, from_b, came_other)
     got_a = along_y(to_a, NEXT_A)
     got_b = along_y(to_b, NEXT_B)
-    piece = join([piece, far], [to_a])
+    piece = join([piece, far], [got_a, got_b])
     beside = ring_x(piece, X_NEXT_B)
 
     index = jnp.arange(64, dtype=jnp.float32)
@@ -381,17 +399,23 @@
     own = finish(where, here, got_a, got_b, k_gain[None, :], cosine, sine)
 
     root = (lax.axis_index("yh") == 0) & (lax.axis_index("z") == 0)
-    have = jnp.where(root, own, jnp.zeros_like(own))
-    for far in ((0, 4), (1, 0), (1, 4)):
-        have = have + along_yh_z(own, [(0, 0) + far])
+    parts = [jnp.where(root, own, jnp.zeros_like(own))]
+    parts += [along_yh_z(own, [(0, 0) + far]) for far in ((1, 0), (0, 2), (0, 6))]
+    have = merge(parts)
     trunk = have
-    for step in (1, -1, 2):
-        trunk = trunk + along_yh_z(
-            have, [(a, b, a, (b + step) % 8) for a in range(2) for b in (0, 4)]
-        )
+    for targets in (
+        ((0, 4), (1, 2), (1, 6), (1, 4)),
+        ((0, 1), (0, 3), (0, 5), (1, 1)),
+        ((0, 7), (1, 3), (1, 5), (1, 7)),
+    ):
+        holders = ((0, 0), (0, 2), (0, 6), (1, 0))
+        trunk = trunk + along_yh_z(have, [a + b for a, b in zip(holders, targets)])
+
     *state, partial = prefix_attend(q, q2, [piece, beside], [have])
-    trunks = [trunk, along_x(trunk, -1), along_x(trunk, 2), along_x(trunk, 1)]
-    return last_attend(where, q, trunks, own, state, ring_x(partial, X_NEXT_A))[None]
+    got = ring_x(partial, X_NEXT_A)
+    opposite = along_x(trunk, 2)
+    trunks = [trunk, along_x(trunk, -1), opposite, along_x(trunk, 1)]
+    return last_attend(where, q, trunks, own, state, got)[None]
 
 
 def solution(mesh):

time: 116 us -> 111 us (0.957)
  the two profiles are of different devices: /device:TPU:8 before, /device:TPU:16 now
where the time goes in v3:
time: 111 us
  starting transfers between devices  73.9 us (67%)
  waiting for transfers between devices  21.7 us (20%)
  Pallas kernels  12.4 us (11%)
  local copies, waits for them, and re-layouts  1.11 us (1%)
    ppermute x5, starting transfers between devices, along_y(): return lax.ppermute(value, Y, pairs)  24.2 us
    ppermute x3, starting transfers between devices, along_z(): return lax.ppermute(value, 'z', [(i, i ^ bit) for i in range(8)])  14.7 us
    ppermute x6, starting transfers between devices, along_yh_z(): lax.ppermute(value, ('yh', 'z'), [(a * 8 + b, c * 8 + d) for a, b, c, d i...  13.4 us
    ppermute x3, starting transfers between devices, along_x(): return lax.ppermute(value, 'x', [(i, (i + s) % 4) for i in range(4)])  9.24 us
    ppermute x3, starting transfers between devices, ring_x(): return lax.ppermute(value, 'x', pairs)  8.42 us
    ppermute x5, waiting for transfers between devices, along_y(): return lax.ppermute(value, Y, pairs)  7.85 us
    ppermute x3, waiting for transfers between devices, along_x(): return lax.ppermute(value, 'x', [(i, (i + s) % 4) for i in range(4)])  6.14 us
    ppermute x3, waiting for transfers between devices, along_z(): return lax.ppermute(value, 'z', [(i, i ^ bit) for i in range(8)])  4.85 us
  transfers between devices with their start and end apart: 22, of which 10 were waited for; matrix products, arithmetic and copies ran while one was open for 0% of the time, Pallas kernels for 6%

profile of v3, /device:TPU:16, one launch (start us, length us, event | category | flops | bytes accessed | tf_op | source)
XLA Modules:
  0.0 110.6 jit_solution(11428648200546103257)
XLA Ops:
  0.0 5.9 %collective-permute-start.1 = (bf16[16,1024]{1,0:T(8,128)(2,1)}, bf16[16,1024]{1,0:T(8,128)(2,1)S(1)}, u32[]{:S(2)}, u32[]{:S(2)}) collective-permute-start(bf16[16,1024]{1,0:T(8,128)(2,1)} %bitcast.16), channel_id=1, source_target_pairs={{0,256},{2,258},{4,260},{6,262},{256,0},{258,2},{260,4},{262,6},{1... | collective-permute-start | bytes 98312 | tf_op jit(solution)/shard_map/ppermute | solution.py:43
  5.9 4.0 %collective-permute-done.1.after_ref.refs_1_ = bf16[16,1024]{1,0:T(8,128)(2,1)S(1)} collective-permute-done((bf16[16,1024]{1,0:T(8,128)(2,1)}, bf16[16,1024]{1,0:T(8,128)(2,1)S(1)}, u32[]{:S(2)}, u32[]{:S(2)}) %collective-permute-start.1) | collective-permute-done | bytes 32800 | tf_op jit(solution)/shard_map/ppermute | solution.py:43
  12.6 3.5 %collective-permute-start.2 = (bf16[3840,128]{1,0:T(8,128)(2,1)S(1)}, bf16[3840,128]{1,0:T(8,128)(2,1)S(1)}, u32[]{:S(2)}, u32[]{:S(2)}) collective-permute-start(bf16[3840,128]{1,0:T(8,128)(2,1)S(1)} %get-tuple-element.14), channel_id=1, source_target_pairs={{0,2},{2,0},{4,6},{6,4},{256,258},{258,256},{260,262},{262,260},{1... | collective-permute-start | bytes 2949128 | tf_op jit(solution)/shard_map/ppermute | solution.py:43
  16.1 6.6 %collective-permute-start.3 = (bf16[3840,128]{1,0:T(8,128)(2,1)S(1)}, bf16[3840,128]{1,0:T(8,128)(2,1)S(1)}, u32[]{:S(2)}, u32[]{:S(2)}) collective-permute-start(bf16[3840,128]{1,0:T(8,128)(2,1)S(1)} %get-tuple-element.15), channel_id=1, source_target_pairs={{0,262},{2,4},{4,2},{6,256},{256,6},{258,260},{260,258},{262,0},{1... | collective-permute-start | bytes 2949128 | tf_op jit(solution)/shard_map/ppermute | solution.py:43
  24.6 7.7 %collective-permute-start.4 = (bf16[32,1024]{1,0:T(8,128)(2,1)S(1)}, bf16[32,1024]{1,0:T(8,128)(2,1)S(1)}, u32[]{:S(2)}, u32[]{:S(2)}) collective-permute-start(bf16[32,1024]{1,0:T(8,128)(2,1)S(1)} %shard_map.65.refs_0_), channel_id=1, source_target_pairs={{0,128},{32,160},{64,192},{96,224},{128,0},{160,32},{192,64},{224,... | collective-permute-start | bytes 196616 | tf_op jit(solution)/shard_map/ppermute | solution.py:47
  32.4 2.4 %collective-permute-done.4.refs_1_ = bf16[32,1024]{1,0:T(8,128)(2,1)S(1)} collective-permute-done((bf16[32,1024]{1,0:T(8,128)(2,1)S(1)}, bf16[32,1024]{1,0:T(8,128)(2,1)S(1)}, u32[]{:S(2)}, u32[]{:S(2)}) %collective-permute-start.4) | collective-permute-done | bytes 65568 | tf_op jit(solution)/shard_map/ppermute | solution.py:47
  34.8 4.9 %collective-permute-start.5 = (bf16[64,1024]{1,0:T(8,128)(2,1)S(1)}, bf16[64,1024]{1,0:T(8,128)(2,1)S(1)}, u32[]{:S(2)}, u32[]{:S(2)}) collective-permute-start(bf16[64,1024]{1,0:T(8,128)(2,1)S(1)} %shard_map.66.refs_0_), channel_id=1, source_target_pairs={{0,64},{32,96},{64,0},{96,32},{128,192},{160,224},{192,128},{224,1... | collective-permute-start | bytes 393224 | tf_op jit(solution)/shard_map/ppermute | solution.py:47
  41.6 2.4 %collective-permute-done.5.refs_1_ = bf16[64,1024]{1,0:T(8,128)(2,1)S(1)} collective-permute-done((bf16[64,1024]{1,0:T(8,128)(2,1)S(1)}, bf16[64,1024]{1,0:T(8,128)(2,1)S(1)}, u32[]{:S(2)}, u32[]{:S(2)}) %collective-permute-start.5) | collective-permute-done | bytes 131104 | tf_op jit(solution)/shard_map/ppermute | solution.py:47
  47.9 2.2 %collective-permute-start.19 = (bf16[128,1024]{1,0:T(8,128)(2,1)S(1)}, bf16[128,1024]{1,0:T(8,128)(2,1)S(1)}, u32[]{:S(2)}, u32[]{:S(2)}) collective-permute-start(bf16[128,1024]{1,0:T(8,128)(2,1)S(1)} %shard_map.67.piece_ref.refs_0_), channel_id=1, source_target_pairs={{0,32},{32,0},{64,96},{96,64},{128,160},{160,128},{192,224},{224,1... | collective-permute-start | bytes 786440 | tf_op jit(solution)/shard_map/ppermute | solution.py:47
  50.5 3.0 %shard_map.69 = (f32[64,768]{1,0:T(8,128)S(1)}, bf16[64,512]{1,0:T(8,128)(2,1)S(1)}, bf16[64,512]{1,0:T(8,128)(2,1)S(1)}) custom-call(s32[4]{0:T(128)S(1)} %pad_add_fusion.where_ref, bf16[64,5120]{1,0:T(8,128)(2,1)S(1)} %bitcast.12, bf16[5120,128]{1,0:T(8,128)(2,1)} %own.1, bf16[5120,128]{1,0:T(8,128)(2,1)} %collective-permute-done.other, ...), custom_call_target="tpu_custom_call" | custom-call | flops 671088640 | bytes 7000000 | tf_op jit(solution)/shard_map/pallas_call | solution.py:175
  53.5 5.9 %collective-permute-start.8 = (bf16[64,512]{1,0:T(8,128)(2,1)S(1)}, bf16[64,512]{1,0:T(8,128)(2,1)S(1)}, u32[]{:S(2)}, u32[]{:S(2)}) collective-permute-start(bf16[64,512]{1,0:T(8,128)(2,1)S(1)} %get-tuple-element.17), channel_id=1, source_target_pairs={{0,2},{2,0},{4,6},{6,4},{256,258},{258,256},{260,262},{262,260},{1... | collective-permute-start | bytes 196616 | tf_op jit(solution)/shard_map/ppermute | solution.py:43
  59.5 2.3 %collective-permute-start.9 = (bf16[64,512]{1,0:T(8,128)(2,1)S(1)}, bf16[64,512]{1,0:T(8,128)(2,1)S(1)}, u32[]{:S(2)}, u32[]{:S(2)}) collective-permute-start(bf16[64,512]{1,0:T(8,128)(2,1)S(1)} %get-tuple-element.18), channel_id=1, source_target_pairs={{0,262},{2,4},{4,2},{6,256},{256,6},{258,260},{260,258},{262,0},{1... | collective-permute-start | bytes 196616 | tf_op jit(solution)/shard_map/ppermute | solution.py:43
  61.9 3.7 %collective-permute-done.9.got_b.refs_3_ = bf16[64,512]{1,0:T(8,128)(2,1)S(1)} collective-permute-done((bf16[64,512]{1,0:T(8,128)(2,1)S(1)}, bf16[64,512]{1,0:T(8,128)(2,1)S(1)}, u32[]{:S(2)}, u32[]{:S(2)}) %collective-permute-start.9) | collective-permute-done | bytes 65568 | tf_op jit(solution)/shard_map/ppermute | solution.py:43
  65.7 4.0 %collective-permute-start.20 = (bf16[256,1024]{1,0:T(8,128)(2,1)S(1)}, bf16[256,1024]{1,0:T(8,128)(2,1)S(1)}, u32[]{:S(2)}, u32[]{:S(2)}) collective-permute-start(bf16[256,1024]{1,0:T(8,128)(2,1)S(1)} %shard_map.72.refs_0_), channel_id=1, source_target_pairs={{0,24},{8,16},{16,8},{24,0},{1,25},{9,17},{17,9},{25,1},{2,26},{10... | collective-permute-start | bytes 1572872 | tf_op jit(solution)/shard_map/ppermute | solution.py:35
  70.8 3.5 %collective-permute-start.10 = (bf16[64,1024]{1,0:T(8,128)(2,1)S(1)}, bf16[64,1024]{1,0:T(8,128)(2,1)S(1)}, u32[]{:S(2)}, u32[]{:S(2)}) collective-permute-start(bf16[64,1024]{1,0:T(8,128)(2,1)S(1)} %shard_map.70.own_ref), channel_id=1, source_target_pairs={{0,256},{1,257},{2,258},{3,259},{4,260},{5,261},{6,262},{7,263},{8... | collective-permute-start | bytes 393224 | tf_op jit(solution)/shard_map/ppermute | solution.py:55
  74.3 2.4 %collective-permute-start.11 = (bf16[64,1024]{1,0:T(8,128)(2,1)S(1)}, bf16[64,1024]{1,0:T(8,128)(2,1)S(1)}, u32[]{:S(2)}, u32[]{:S(2)}) collective-permute-start(bf16[64,1024]{1,0:T(8,128)(2,1)S(1)} %shard_map.70.own_ref), channel_id=1, source_target_pairs={{0,64},{1,65},{2,66},{3,67},{4,68},{5,69},{6,70},{7,71},{8,72},{9,... | collective-permute-start | bytes 393224 | tf_op jit(solution)/shard_map/ppermute | solution.py:55
  76.8 3.6 %collective-permute-start.12 = (bf16[64,1024]{1,0:T(8,128)(2,1)S(1)}, bf16[64,1024]{1,0:T(8,128)(2,1)S(1)}, u32[]{:S(2)}, u32[]{:S(2)}) collective-permute-start(bf16[64,1024]{1,0:T(8,128)(2,1)S(1)} %shard_map.70.own_ref), channel_id=1, source_target_pairs={{0,192},{1,193},{2,194},{3,195},{4,196},{5,197},{6,198},{7,199},{8... | collective-permute-start | bytes 393224 | tf_op jit(solution)/shard_map/ppermute | solution.py:55
  80.4 2.4 %collective-permute-done.12.refs_3_ = bf16[64,1024]{1,0:T(8,128)(2,1)S(1)} collective-permute-done((bf16[64,1024]{1,0:T(8,128)(2,1)S(1)}, bf16[64,1024]{1,0:T(8,128)(2,1)S(1)}, u32[]{:S(2)}, u32[]{:S(2)}) %collective-permute-start.12) | collective-permute-done | bytes 131104 | tf_op jit(solution)/shard_map/ppermute | solution.py:55
  89.0 2.5 %collective-permute-start.21 = (bf16[64,2944]{1,0:T(8,128)(2,1)S(1)}, bf16[64,2944]{1,0:T(8,128)(2,1)S(1)}, u32[]{:S(2)}, u32[]{:S(2)}) collective-permute-start(bf16[64,2944]{1,0:T(8,128)(2,1)S(1)} %get-tuple-element.22), channel_id=1, source_target_pairs={{0,8},{8,0},{16,24},{24,16},{1,9},{9,1},{17,25},{25,17},{2,10},{10... | collective-permute-start | bytes 1130504 | tf_op jit(solution)/shard_map/ppermute | solution.py:35
  91.5 2.5 %collective-permute-start.16 = (bf16[64,1024]{1,0:T(8,128)(2,1)S(1)}, bf16[64,1024]{1,0:T(8,128)(2,1)S(1)}, u32[]{:S(2)}, u32[]{:S(2)}) collective-permute-start(bf16[64,1024]{1,0:T(8,128)(2,1)S(1)} %add_add_fusion.t0), channel_id=1, source_target_pairs={{0,24},{8,0},{16,8},{24,16},{1,25},{9,1},{17,9},{25,17},{2,26},{10... | collective-permute-start | bytes 393224 | tf_op jit(solution)/shard_map/ppermute | solution.py:39
  94.1 4.8 %collective-permute-start.17 = (bf16[64,1024]{1,0:T(8,128)(2,1)S(1)}, bf16[64,1024]{1,0:T(8,128)(2,1)S(1)}, u32[]{:S(2)}, u32[]{:S(2)}) collective-permute-start(bf16[64,1024]{1,0:T(8,128)(2,1)S(1)} %add_add_fusion.t0), channel_id=1, source_target_pairs={{0,16},{8,24},{16,0},{24,8},{1,17},{9,25},{17,1},{25,9},{2,18},{10... | collective-permute-start | bytes 393224 | tf_op jit(solution)/shard_map/ppermute | solution.py:39
  100.8 2.6 %collective-permute-done.16.t1 = bf16[64,1024]{1,0:T(8,128)(2,1)S(1)} collective-permute-done((bf16[64,1024]{1,0:T(8,128)(2,1)S(1)}, bf16[64,1024]{1,0:T(8,128)(2,1)S(1)}, u32[]{:S(2)}, u32[]{:S(2)}) %collective-permute-start.16) | collective-permute-done | bytes 131104 | tf_op jit(solution)/shard_map/ppermute | solution.py:39
  104.1 2.9 %collective-permute-done.18.t3 = bf16[64,1024]{1,0:T(8,128)(2,1)S(1)} collective-permute-done((bf16[64,1024]{1,0:T(8,128)(2,1)S(1)}, bf16[64,1024]{1,0:T(8,128)(2,1)S(1)}, u32[]{:S(2)}, u32[]{:S(2)}) %collective-permute-start.18) | collective-permute-done | bytes 131104 | tf_op jit(solution)/shard_map/ppermute | solution.py:39
  107.0 3.6 %shard_map.74 = bf16[64,2560]{1,0:T(8,128)(2,1)} custom-call(s32[4]{0:T(128)S(1)} %pad_add_fusion.where_ref, bf16[64,2560]{1,0:T(8,128)(2,1)S(1)} %bitcast.15, bf16[64,1024]{1,0:T(8,128)(2,1)S(1)} %add_add_fusion.t0, bf16[64,1024]{1,0:T(8,128)(2,1)S(1)} %collective-permute-done.16.t1, bf16[64,1024]{1,0:T(8,128)(2,1)S(1)} %collective-permute-done.17.t2, ...), custom_call_target="tpu_custom_call" | custom-call | flops 83886080 | bytes 3000000 | tf_op jit(solution)/shard_map/pallas_call | solution.py:352
  (48 shorter events, 20.2 us)
Async XLA Ops:
  0.0 9.9 %collective-permute-start.1 = (bf16[16,1024]{1,0:T(8,128)(2,1)}, bf16[16,1024]{1,0:T(8,128)(2,1)S(1)}, u32[]{:S(2)}, u32[]{:S(2)}) collective-permute-start(bf16[16,1024]{1,0:T(8,128)(2,1)} %bitcast.16), channel_id=1, source_target_pairs={{0,256},{2,258},{4,260},{6,262},{256,0},{258,2},{260,4},{262,6},{1... | collective-permute-start | bytes 98312 | tf_op jit(solution)/shard_map/ppermute | solution.py:43
  11.0 13.6 %copy-start.3 = (bf16[1,16,1024]{2,1,0:T(8,128)(2,1)S(1)}, bf16[1,16,1024]{2,1,0:T(8,128)(2,1)}, u32[]{:S(2)}) copy-start(bf16[1,16,1024]{2,1,0:T(8,128)(2,1)} %param.10) | copy-start | bytes 98308
  12.6 31.5 %collective-permute-start.2 = (bf16[3840,128]{1,0:T(8,128)(2,1)S(1)}, bf16[3840,128]{1,0:T(8,128)(2,1)S(1)}, u32[]{:S(2)}, u32[]{:S(2)}) collective-permute-start(bf16[3840,128]{1,0:T(8,128)(2,1)S(1)} %get-tuple-element.14), channel_id=1, source_target_pairs={{0,2},{2,0},{4,6},{6,4},{256,258},{258,256},{260,262},{262,260},{1... | collective-permute-start | bytes 2949128 | tf_op jit(solution)/shard_map/ppermute | solution.py:43
  16.1 28.0 %collective-permute-start.3 = (bf16[3840,128]{1,0:T(8,128)(2,1)S(1)}, bf16[3840,128]{1,0:T(8,128)(2,1)S(1)}, u32[]{:S(2)}, u32[]{:S(2)}) collective-permute-start(bf16[3840,128]{1,0:T(8,128)(2,1)S(1)} %get-tuple-element.15), channel_id=1, source_target_pairs={{0,262},{2,4},{4,2},{6,256},{256,6},{258,260},{260,258},{262,0},{1... | collective-permute-start | bytes 2949128 | tf_op jit(solution)/shard_map/ppermute | solution.py:43
  22.7 21.4 %collective-permute-start.6 = (bf16[64,2560]{1,0:T(8,128)(2,1)S(1)}, bf16[64,2560]{1,0:T(8,128)(2,1)S(1)}, u32[]{:S(2)}, u32[]{:S(2)}) collective-permute-start(bf16[64,2560]{1,0:T(8,128)(2,1)S(1)} %bitcast.13), channel_id=1, source_target_pairs={{0,8},{8,0},{16,24},{24,16},{1,9},{9,1},{17,25},{25,17},{2,10},{10... | collective-permute-start | bytes 983048 | tf_op jit(solution)/shard_map/ppermute | solution.py:35
  24.6 10.2 %collective-permute-start.4 = (bf16[32,1024]{1,0:T(8,128)(2,1)S(1)}, bf16[32,1024]{1,0:T(8,128)(2,1)S(1)}, u32[]{:S(2)}, u32[]{:S(2)}) collective-permute-start(bf16[32,1024]{1,0:T(8,128)(2,1)S(1)} %shard_map.65.refs_0_), channel_id=1, source_target_pairs={{0,128},{32,160},{64,192},{96,224},{128,0},{160,32},{192,64},{224,... | collective-permute-start | bytes 196616 | tf_op jit(solution)/shard_map/ppermute | solution.py:47
  34.8 9.2 %collective-permute-start.5 = (bf16[64,1024]{1,0:T(8,128)(2,1)S(1)}, bf16[64,1024]{1,0:T(8,128)(2,1)S(1)}, u32[]{:S(2)}, u32[]{:S(2)}) collective-permute-start(bf16[64,1024]{1,0:T(8,128)(2,1)S(1)} %shard_map.66.refs_0_), channel_id=1, source_target_pairs={{0,64},{32,96},{64,0},{96,32},{128,192},{160,224},{192,128},{224,1... | collective-permute-start | bytes 393224 | tf_op jit(solution)/shard_map/ppermute | solution.py:47
  39.7 10.4 %collective-permute-start = (bf16[5120,128]{1,0:T(8,128)(2,1)}, bf16[5120,128]{1,0:T(8,128)(2,1)}, u32[]{:S(2)}, u32[]{:S(2)}) collective-permute-start(bf16[5120,128]{1,0:T(8,128)(2,1)} %own.1), channel_id=1, source_target_pairs={{0,1},{1,0},{2,3},{3,2},{4,5},{5,4},{6,7},{7,6},{8,9},{9,8},{10,11... | collective-permute-start | bytes 3932168 | tf_op jit(solution)/shard_map/ppermute | solution.py:51
  45.3 5.3 %collective-permute-start.7 = (bf16[5120,128]{1,0:T(8,128)(2,1)}, bf16[5120,128]{1,0:T(8,128)(2,1)}, u32[]{:S(2)}, u32[]{:S(2)}) collective-permute-start(bf16[5120,128]{1,0:T(8,128)(2,1)} %shard_map.68), channel_id=1, source_target_pairs={{0,1},{1,0},{2,3},{3,2},{4,5},{5,4},{6,7},{7,6},{8,9},{9,8},{10,11... | collective-permute-start | bytes 3932168 | tf_op jit(solution)/shard_map/ppermute | solution.py:51
  47.9 13.9 %collective-permute-start.19 = (bf16[128,1024]{1,0:T(8,128)(2,1)S(1)}, bf16[128,1024]{1,0:T(8,128)(2,1)S(1)}, u32[]{:S(2)}, u32[]{:S(2)}) collective-permute-start(bf16[128,1024]{1,0:T(8,128)(2,1)S(1)} %shard_map.67.piece_ref.refs_0_), channel_id=1, source_target_pairs={{0,32},{32,0},{64,96},{96,64},{128,160},{160,128},{192,224},{224,1... | collective-permute-start | bytes 786440 | tf_op jit(solution)/shard_map/ppermute | solution.py:47
  53.5 16.5 %copy-start.4 = (f32[512]{0:T(512)S(1)}, f32[512]{0:T(512)}, u32[]{:S(2)}) copy-start(f32[512]{0:T(512)} %param.8) | copy-start | bytes 6148
  53.5 8.4 %collective-permute-start.8 = (bf16[64,512]{1,0:T(8,128)(2,1)S(1)}, bf16[64,512]{1,0:T(8,128)(2,1)S(1)}, u32[]{:S(2)}, u32[]{:S(2)}) collective-permute-start(bf16[64,512]{1,0:T(8,128)(2,1)S(1)} %get-tuple-element.17), channel_id=1, source_target_pairs={{0,2},{2,0},{4,6},{6,4},{256,258},{258,256},{260,262},{262,260},{1... | collective-permute-start | bytes 196616 | tf_op jit(solution)/shard_map/ppermute | solution.py:43
  59.5 6.2 %collective-permute-start.9 = (bf16[64,512]{1,0:T(8,128)(2,1)S(1)}, bf16[64,512]{1,0:T(8,128)(2,1)S(1)}, u32[]{:S(2)}, u32[]{:S(2)}) collective-permute-start(bf16[64,512]{1,0:T(8,128)(2,1)S(1)} %get-tuple-element.18), channel_id=1, source_target_pairs={{0,262},{2,4},{4,2},{6,256},{256,6},{258,260},{260,258},{262,0},{1... | collective-permute-start | bytes 196616 | tf_op jit(solution)/shard_map/ppermute | solution.py:43
  65.7 21.2 %collective-permute-start.20 = (bf16[256,1024]{1,0:T(8,128)(2,1)S(1)}, bf16[256,1024]{1,0:T(8,128)(2,1)S(1)}, u32[]{:S(2)}, u32[]{:S(2)}) collective-permute-start(bf16[256,1024]{1,0:T(8,128)(2,1)S(1)} %shard_map.72.refs_0_), channel_id=1, source_target_pairs={{0,24},{8,16},{16,8},{24,0},{1,25},{9,17},{17,9},{25,1},{2,26},{10... | collective-permute-start | bytes 1572872 | tf_op jit(solution)/shard_map/ppermute | solution.py:35
  70.8 9.6 %collective-permute-start.10 = (bf16[64,1024]{1,0:T(8,128)(2,1)S(1)}, bf16[64,1024]{1,0:T(8,128)(2,1)S(1)}, u32[]{:S(2)}, u32[]{:S(2)}) collective-permute-start(bf16[64,1024]{1,0:T(8,128)(2,1)S(1)} %shard_map.70.own_ref), channel_id=1, source_target_pairs={{0,256},{1,257},{2,258},{3,259},{4,260},{5,261},{6,262},{7,263},{8... | collective-permute-start | bytes 393224 | tf_op jit(solution)/shard_map/ppermute | solution.py:55
  74.3 6.0 %collective-permute-start.11 = (bf16[64,1024]{1,0:T(8,128)(2,1)S(1)}, bf16[64,1024]{1,0:T(8,128)(2,1)S(1)}, u32[]{:S(2)}, u32[]{:S(2)}) collective-permute-start(bf16[64,1024]{1,0:T(8,128)(2,1)S(1)} %shard_map.70.own_ref), channel_id=1, source_target_pairs={{0,64},{1,65},{2,66},{3,67},{4,68},{5,69},{6,70},{7,71},{8,72},{9,... | collective-permute-start | bytes 393224 | tf_op jit(solution)/shard_map/ppermute | solution.py:55
  76.8 6.1 %collective-permute-start.12 = (bf16[64,1024]{1,0:T(8,128)(2,1)S(1)}, bf16[64,1024]{1,0:T(8,128)(2,1)S(1)}, u32[]{:S(2)}, u32[]{:S(2)}) collective-permute-start(bf16[64,1024]{1,0:T(8,128)(2,1)S(1)} %shard_map.70.own_ref), channel_id=1, source_target_pairs={{0,192},{1,193},{2,194},{3,195},{4,196},{5,197},{6,198},{7,199},{8... | collective-permute-start | bytes 393224 | tf_op jit(solution)/shard_map/ppermute | solution.py:55
  82.9 8.6 %collective-permute-start.13 = (bf16[64,1024]{1,0:T(8,128)(2,1)S(1)}, bf16[64,1024]{1,0:T(8,128)(2,1)S(1)}, u32[]{:S(2)}, u32[]{:S(2)}) collective-permute-start(bf16[64,1024]{1,0:T(8,128)(2,1)S(1)} %shard_map.71.refs_2_), channel_id=1, source_target_pairs={{0,128},{64,320},{192,448},{256,384},{1,129},{65,321},{193,449},{2... | collective-permute-start | bytes 393224 | tf_op jit(solution)/shard_map/ppermute | solution.py:55
  84.2 7.3 %collective-permute-start.14 = (bf16[64,1024]{1,0:T(8,128)(2,1)S(1)}, bf16[64,1024]{1,0:T(8,128)(2,1)S(1)}, u32[]{:S(2)}, u32[]{:S(2)}) collective-permute-start(bf16[64,1024]{1,0:T(8,128)(2,1)S(1)} %shard_map.71.refs_2_), channel_id=1, source_target_pairs={{0,32},{64,96},{192,160},{256,288},{1,33},{65,97},{193,161},{257,2... | collective-permute-start | bytes 393224 | tf_op jit(solution)/shard_map/ppermute | solution.py:55
  85.5 6.0 %collective-permute-start.15 = (bf16[64,1024]{1,0:T(8,128)(2,1)S(1)}, bf16[64,1024]{1,0:T(8,128)(2,1)S(1)}, u32[]{:S(2)}, u32[]{:S(2)}) collective-permute-start(bf16[64,1024]{1,0:T(8,128)(2,1)S(1)} %shard_map.71.refs_2_), channel_id=1, source_target_pairs={{0,224},{64,352},{192,416},{256,480},{1,225},{65,353},{193,417},{2... | collective-permute-start | bytes 393224 | tf_op jit(solution)/shard_map/ppermute | solution.py:55
  89.0 18.0 %collective-permute-start.21 = (bf16[64,2944]{1,0:T(8,128)(2,1)S(1)}, bf16[64,2944]{1,0:T(8,128)(2,1)S(1)}, u32[]{:S(2)}, u32[]{:S(2)}) collective-permute-start(bf16[64,2944]{1,0:T(8,128)(2,1)S(1)} %get-tuple-element.22), channel_id=1, source_target_pairs={{0,8},{8,0},{16,24},{24,16},{1,9},{9,1},{17,25},{25,17},{2,10},{10... | collective-permute-start | bytes 1130504 | tf_op jit(solution)/shard_map/ppermute | solution.py:35
  91.5 11.9 %collective-permute-start.16 = (bf16[64,1024]{1,0:T(8,128)(2,1)S(1)}, bf16[64,1024]{1,0:T(8,128)(2,1)S(1)}, u32[]{:S(2)}, u32[]{:S(2)}) collective-permute-start(bf16[64,1024]{1,0:T(8,128)(2,1)S(1)} %add_add_fusion.t0), channel_id=1, source_target_pairs={{0,24},{8,0},{16,8},{24,16},{1,25},{9,1},{17,9},{25,17},{2,26},{10... | collective-permute-start | bytes 393224 | tf_op jit(solution)/shard_map/ppermute | solution.py:39
  94.1 10.0 %collective-permute-start.17 = (bf16[64,1024]{1,0:T(8,128)(2,1)S(1)}, bf16[64,1024]{1,0:T(8,128)(2,1)S(1)}, u32[]{:S(2)}, u32[]{:S(2)}) collective-permute-start(bf16[64,1024]{1,0:T(8,128)(2,1)S(1)} %add_add_fusion.t0), channel_id=1, source_target_pairs={{0,16},{8,24},{16,0},{24,8},{1,17},{9,25},{17,1},{25,9},{2,18},{10... | collective-permute-start | bytes 393224 | tf_op jit(solution)/shard_map/ppermute | solution.py:39
  98.9 8.1 %collective-permute-start.18 = (bf16[64,1024]{1,0:T(8,128)(2,1)S(1)}, bf16[64,1024]{1,0:T(8,128)(2,1)S(1)}, u32[]{:S(2)}, u32[]{:S(2)}) collective-permute-start(bf16[64,1024]{1,0:T(8,128)(2,1)S(1)} %add_add_fusion.t0), channel_id=1, source_target_pairs={{0,8},{8,16},{16,24},{24,0},{1,9},{9,17},{17,25},{25,1},{2,10},{10... | collective-permute-start | bytes 393224 | tf_op jit(solution)/shard_map/ppermute | solution.py:39
  (3 other events, 19.2 us)

commit v4 on v3

--- a/solution.py
+++ b/solution.py
@@ -247,38 +247,36 @@
     )(*parts)
 
 
-def prefix_kernel(n, q_ref, q2_ref, *refs):
-    blocks, (high_ref, total_ref, sum_ref, send_ref) = refs[:n], refs[-4:]
+def attend_prefix(q, blocks, g):
+    high = total = acc = None
+    for block in blocks:
+        s = scores(q, block[:, g * HEAD : (g + 1) * HEAD])
+        v = block[:, KEY_WIDTH + g * HEAD : KEY_WIDTH + (g + 1) * HEAD]
+        top = jnp.max(s, axis=-1, keepdims=True)
+        new = top if high is None else jnp.maximum(high, top)
+        p = jnp.exp2(s - new)
+        part = jnp.sum(p, axis=-1, keepdims=True)
+        pv = jnp.dot(p.astype(jnp.bfloat16), v, preferred_element_type=jnp.float32)
+        if high is None:
+            total, acc = part, pv
+        else:
+            factor = jnp.exp2(high - new)
+            total, acc = total * factor + part, acc * factor + pv
+        high = new
+    return high, total, acc
+
+
+def partner_kernel(q_ref, one_ref, two_ref, after_ref, send_ref):
     lane = lax.broadcasted_iota(jnp.int32, (ROWS, HEAD), 1)
     logs = jnp.zeros((ROWS, HEAD), jnp.float32)
-
-    def attend(q, g):
-        high = total = acc = None
-        for block in blocks:
-            s = scores(q, block[:, g * HEAD : (g + 1) * HEAD])
-            v = block[:, KEY_WIDTH + g * HEAD : KEY_WIDTH + (g + 1) * HEAD]
-            top = jnp.max(s, axis=-1, keepdims=True)
-            new = top if high is None else jnp.maximum(high, top)
-            p = jnp.exp2(s - new)
-            part = jnp.sum(p, axis=-1, keepdims=True)
-            pv = jnp.dot(p.astype(jnp.bfloat16), v, preferred_element_type=jnp.float32)
-            if high is None:
-                total, acc = part, pv
-            else:
-                factor = jnp.exp2(high - new)
-                total, acc = total * factor + part, acc * factor + pv
-            high = new
-        return high, total, acc
-
     for g in range(HEADS_KV):
-        high, total, acc = attend(queries(q2_ref, g), g)
+        high, total, acc = attend_prefix(queries(q_ref, g), [one_ref, two_ref], g)
         acc = (acc * (1.0 / total)).astype(jnp.bfloat16)
         log = high + jnp.log2(total)
         for j in range(GROUP):
             h = g * GROUP + j
             send_ref[:, h * HEAD : (h + 1) * HEAD] = acc[j * ROWS : (j + 1) * ROWS]
             logs = jnp.where(lane == h, log[j * ROWS : (j + 1) * ROWS], logs)
-        high_ref[g], total_ref[g], sum_ref[g] = attend(queries(q_ref, g), g)
     for part in range(3):
         at = (20 + part) * HEAD
         piece = logs.astype(jnp.bfloat16)
@@ -286,23 +284,31 @@
         logs = logs - piece.astype(jnp.float32)
 
 
-def prefix_attend(q, q2, blocks, after):
-    n = len(blocks)
-    m = ROWS * GROUP
-    keys = 2 * sum(b.shape[0] for b in blocks)
-    return pl.pallas_call(
-        functools.partial(prefix_kernel, n),
-        out_shape=[
-            jax.ShapeDtypeStruct((HEADS_KV, m, 1), jnp.float32),
-            jax.ShapeDtypeStruct((HEADS_KV, m, 1), jnp.float32),
-            jax.ShapeDtypeStruct((HEADS_KV, m, HEAD), jnp.float32),
-            jax.ShapeDtypeStruct((ROWS, 23 * HEAD), jnp.bfloat16),
-        ],
-        in_specs=[VM] * (n + 2) + [ANY] * len(after),
-        out_specs=[VM] * 4,
-        compiler_params=PARAMS,
-        cost_estimate=cost(4 * 1280 * keys * 128, keys * 2048 + 2000000, 1280 * keys),
-    )(q, q2, *blocks, *after)
+def own_kernel(q_ref, one_ref, two_ref, after_ref, high_ref, total_ref, sum_ref):
+    for g in range(HEADS_KV):
+        high_ref[g], total_ref[g], sum_ref[g] = attend_prefix(
+            queries(q_ref, g), [one_ref, two_ref], g
+        )
+
+
+def prefix_attend(kernel, out_shape, q, one, two, after):
+    keys = one.shape[0] + two.shape[0]
+    return pl.pallas_call(
+        kernel,
+        out_shape=out_shape,
+        in_specs=[VM] * 3 + [ANY],
+        out_specs=[VM] * len(out_shape),
+        compiler_params=PARAMS,
+        cost_estimate=cost(4 * 1280 * keys * 128, keys * 2048 + 1000000, 1280 * keys),
+    )(q, one, two, after)
+
+
+PARTIAL = [jax.ShapeDtypeStruct((ROWS, 23 * HEAD), jnp.bfloat16)]
+STATE = [
+    jax.ShapeDtypeStruct((HEADS_KV, ROWS * GROUP, 1), jnp.float32),
+    jax.ShapeDtypeStruct((HEADS_KV, ROWS * GROUP, 1), jnp.float32),
+    jax.ShapeDtypeStruct((HEADS_KV, ROWS * GROUP, HEAD), jnp.float32),
+]
 
 
 def last_kernel(
@@ -411,7 +417,8 @@
         holders = ((0, 0), (0, 2), (0, 6), (1, 0))
         trunk = trunk + along_yh_z(have, [a + b for a, b in zip(holders, targets)])
 
-    *state, partial = prefix_attend(q, q2, [piece, beside], [have])
+    (partial,) = prefix_attend(partner_kernel, PARTIAL, q2, piece, beside, have)
+    state = prefix_attend(own_kernel, STATE, q, piece, beside, trunk)
     got = ring_x(partial, X_NEXT_A)
     opposite = along_x(trunk, 2)
     trunks = [trunk, along_x(trunk, -1), opposite, along_x(trunk, 1)]

time: 111 us -> 112 us (level)
  the two profiles are of different devices: /device:TPU:16 before, /device:TPU:368 now
where the time goes in v4:
time: 112 us; the launch traced here: 111 us
  starting transfers between devices  51.8 us (46%)
  waiting for transfers between devices  43.3 us (39%)
  Pallas kernels  12.7 us (11%)
  local copies, waits for them, and re-layouts  2.04 us (2%)
    ppermute x5, starting transfers between devices, along_y(): return lax.ppermute(value, Y, pairs)  15.3 us
    ppermute x6, waiting for transfers between devices, along_yh_z(): lax.ppermute(value, ('yh', 'z'), [(a * 8 + b, c * 8 + d) for a, b, c, d i...  13.5 us
    ppermute x3, starting transfers between devices, along_z(): return lax.ppermute(value, 'z', [(i, i ^ bit) for i in range(8)])  10.4 us
    ppermute x3, waiting for transfers between devices, along_z(): return lax.ppermute(value, 'z', [(i, i ^ bit) for i in range(8)])  10.1 us
    ppermute x5, waiting for transfers between devices, along_y(): return lax.ppermute(value, Y, pairs)  9.57 us
    ppermute x3, starting transfers between devices, ring_x(): return lax.ppermute(value, 'x', pairs)  9.32 us
    ppermute x3, starting transfers between devices, along_x(): return lax.ppermute(value, 'x', [(i, (i + s) % 4) for i in range(4)])  8.39 us
    ppermute x3, waiting for transfers between devices, ring_x(): return lax.ppermute(value, 'x', pairs)  5.13 us
  transfers between devices with their start and end apart: 22, of which 9 were waited for; matrix products, arithmetic and copies ran while one was open for 0% of the time, Pallas kernels for 7%

profile of v4, /device:TPU:368, one launch (start us, length us, event | category | flops | bytes accessed | tf_op | source)
XLA Modules:
  0.0 111.4 jit_solution(11145194268936190418)
XLA Ops:
  0.0 3.8 %collective-permute-start.1 = (bf16[16,1024]{1,0:T(8,128)(2,1)}, bf16[16,1024]{1,0:T(8,128)(2,1)S(1)}, u32[]{:S(2)}, u32[]{:S(2)}) collective-permute-start(bf16[16,1024]{1,0:T(8,128)(2,1)} %bitcast.16), channel_id=1, source_target_pairs={{0,256},{2,258},{4,260},{6,262},{256,0},{258,2},{260,4},{262,6},{1... | collective-permute-start | bytes 98312 | tf_op jit(solution)/shard_map/ppermute | solution.py:43
  3.8 6.1 %collective-permute-done.1.after_ref.refs_1_ = bf16[16,1024]{1,0:T(8,128)(2,1)S(1)} collective-permute-done((bf16[16,1024]{1,0:T(8,128)(2,1)}, bf16[16,1024]{1,0:T(8,128)(2,1)S(1)}, u32[]{:S(2)}, u32[]{:S(2)}) %collective-permute-start.1) | collective-permute-done | bytes 32800 | tf_op jit(solution)/shard_map/ppermute | solution.py:43
  12.6 2.9 %collective-permute-start.2 = (bf16[3840,128]{1,0:T(8,128)(2,1)S(1)}, bf16[3840,128]{1,0:T(8,128)(2,1)S(1)}, u32[]{:S(2)}, u32[]{:S(2)}) collective-permute-start(bf16[3840,128]{1,0:T(8,128)(2,1)S(1)} %get-tuple-element.13), channel_id=1, source_target_pairs={{0,2},{2,0},{4,6},{6,4},{256,258},{258,256},{260,262},{262,260},{1... | collective-permute-start | bytes 2949128 | tf_op jit(solution)/shard_map/ppermute | solution.py:43
  15.5 3.8 %collective-permute-start.3 = (bf16[3840,128]{1,0:T(8,128)(2,1)S(1)}, bf16[3840,128]{1,0:T(8,128)(2,1)S(1)}, u32[]{:S(2)}, u32[]{:S(2)}) collective-permute-start(bf16[3840,128]{1,0:T(8,128)(2,1)S(1)} %get-tuple-element.14), channel_id=1, source_target_pairs={{0,262},{2,4},{4,2},{6,256},{256,6},{258,260},{260,258},{262,0},{1... | collective-permute-start | bytes 2949128 | tf_op jit(solution)/shard_map/ppermute | solution.py:43
  19.4 3.4 %collective-permute-start.6 = (bf16[64,2560]{1,0:T(8,128)(2,1)S(1)}, bf16[64,2560]{1,0:T(8,128)(2,1)S(1)}, u32[]{:S(2)}, u32[]{:S(2)}) collective-permute-start(bf16[64,2560]{1,0:T(8,128)(2,1)S(1)} %bitcast.13), channel_id=1, source_target_pairs={{0,8},{8,0},{16,24},{24,16},{1,9},{9,1},{17,25},{25,17},{2,10},{10... | collective-permute-start | bytes 983048 | tf_op jit(solution)/shard_map/ppermute | solution.py:35
  22.8 1.9 %collective-permute-start.4 = (bf16[32,1024]{1,0:T(8,128)(2,1)S(1)}, bf16[32,1024]{1,0:T(8,128)(2,1)S(1)}, u32[]{:S(2)}, u32[]{:S(2)}) collective-permute-start(bf16[32,1024]{1,0:T(8,128)(2,1)S(1)} %shard_map.65.refs_0_), channel_id=1, source_target_pairs={{0,128},{32,160},{64,192},{96,224},{128,0},{160,32},{192,64},{224,... | collective-permute-start | bytes 196616 | tf_op jit(solution)/shard_map/ppermute | solution.py:47
  24.7 8.1 %collective-permute-done.4.refs_1_ = bf16[32,1024]{1,0:T(8,128)(2,1)S(1)} collective-permute-done((bf16[32,1024]{1,0:T(8,128)(2,1)S(1)}, bf16[32,1024]{1,0:T(8,128)(2,1)S(1)}, u32[]{:S(2)}, u32[]{:S(2)}) %collective-permute-start.4) | collective-permute-done | bytes 65568 | tf_op jit(solution)/shard_map/ppermute | solution.py:47
  32.9 4.3 %collective-permute-start.5 = (bf16[64,1024]{1,0:T(8,128)(2,1)S(1)}, bf16[64,1024]{1,0:T(8,128)(2,1)S(1)}, u32[]{:S(2)}, u32[]{:S(2)}) collective-permute-start(bf16[64,1024]{1,0:T(8,128)(2,1)S(1)} %shard_map.66.refs_0_), channel_id=1, source_target_pairs={{0,64},{32,96},{64,0},{96,32},{128,192},{160,224},{192,128},{224,1... | collective-permute-start | bytes 393224 | tf_op jit(solution)/shard_map/ppermute | solution.py:47
  37.2 1.9 %collective-permute-start = (bf16[5120,128]{1,0:T(8,128)(2,1)}, bf16[5120,128]{1,0:T(8,128)(2,1)}, u32[]{:S(2)}, u32[]{:S(2)}) collective-permute-start(bf16[5120,128]{1,0:T(8,128)(2,1)} %own.1), channel_id=1, source_target_pairs={{0,1},{1,0},{2,3},{3,2},{4,5},{5,4},{6,7},{7,6},{8,9},{9,8},{10,11... | collective-permute-start | bytes 3932168 | tf_op jit(solution)/shard_map/ppermute | solution.py:51
  39.1 1.9 %collective-permute-done.5.refs_1_ = bf16[64,1024]{1,0:T(8,128)(2,1)S(1)} collective-permute-done((bf16[64,1024]{1,0:T(8,128)(2,1)S(1)}, bf16[64,1024]{1,0:T(8,128)(2,1)S(1)}, u32[]{:S(2)}, u32[]{:S(2)}) %collective-permute-start.5) | collective-permute-done | bytes 131104 | tf_op jit(solution)/shard_map/ppermute | solution.py:47
  44.9 4.1 %collective-permute-start.19 = (bf16[128,1024]{1,0:T(8,128)(2,1)S(1)}, bf16[128,1024]{1,0:T(8,128)(2,1)S(1)}, u32[]{:S(2)}, u32[]{:S(2)}) collective-permute-start(bf16[128,1024]{1,0:T(8,128)(2,1)S(1)} %shard_map.67.piece_ref.refs_0_), channel_id=1, source_target_pairs={{0,32},{32,0},{64,96},{96,64},{128,160},{160,128},{192,224},{224,1... | collective-permute-start | bytes 786440 | tf_op jit(solution)/shard_map/ppermute | solution.py:47
  49.1 3.0 %shard_map.69 = (f32[64,768]{1,0:T(8,128)S(1)}, bf16[64,512]{1,0:T(8,128)(2,1)S(1)}, bf16[64,512]{1,0:T(8,128)(2,1)S(1)}) custom-call(s32[4]{0:T(128)S(1)} %pad_add_fusion.where_ref, bf16[64,5120]{1,0:T(8,128)(2,1)S(1)} %bitcast.12, bf16[5120,128]{1,0:T(8,128)(2,1)} %own.1, bf16[5120,128]{1,0:T(8,128)(2,1)} %collective-permute-done.other, ...), custom_call_target="tpu_custom_call" | custom-call | flops 671088640 | bytes 7000000 | tf_op jit(solution)/shard_map/pallas_call | solution.py:175
  52.2 2.1 %collective-permute-start.8 = (bf16[64,512]{1,0:T(8,128)(2,1)S(1)}, bf16[64,512]{1,0:T(8,128)(2,1)S(1)}, u32[]{:S(2)}, u32[]{:S(2)}) collective-permute-start(bf16[64,512]{1,0:T(8,128)(2,1)S(1)} %get-tuple-element.16), channel_id=1, source_target_pairs={{0,2},{2,0},{4,6},{6,4},{256,258},{258,256},{260,262},{262,260},{1... | collective-permute-start | bytes 196616 | tf_op jit(solution)/shard_map/ppermute | solution.py:43
  54.2 2.7 %collective-permute-start.9 = (bf16[64,512]{1,0:T(8,128)(2,1)S(1)}, bf16[64,512]{1,0:T(8,128)(2,1)S(1)}, u32[]{:S(2)}, u32[]{:S(2)}) collective-permute-start(bf16[64,512]{1,0:T(8,128)(2,1)S(1)} %get-tuple-element.17), channel_id=1, source_target_pairs={{0,262},{2,4},{4,2},{6,256},{256,6},{258,260},{260,258},{262,0},{1... | collective-permute-start | bytes 196616 | tf_op jit(solution)/shard_map/ppermute | solution.py:43
  58.5 1.9 %collective-permute-done.9.got_b.refs_3_ = bf16[64,512]{1,0:T(8,128)(2,1)S(1)} collective-permute-done((bf16[64,512]{1,0:T(8,128)(2,1)S(1)}, bf16[64,512]{1,0:T(8,128)(2,1)S(1)}, u32[]{:S(2)}, u32[]{:S(2)}) %collective-permute-start.9) | collective-permute-done | bytes 65568 | tf_op jit(solution)/shard_map/ppermute | solution.py:43
  60.4 4.0 %collective-permute-start.20 = (bf16[256,1024]{1,0:T(8,128)(2,1)S(1)}, bf16[256,1024]{1,0:T(8,128)(2,1)S(1)}, u32[]{:S(2)}, u32[]{:S(2)}) collective-permute-start(bf16[256,1024]{1,0:T(8,128)(2,1)S(1)} %shard_map.72.one_ref), channel_id=1, source_target_pairs={{0,24},{8,16},{16,8},{24,0},{1,25},{9,17},{17,9},{25,1},{2,26},{10... | collective-permute-start | bytes 1572872 | tf_op jit(solution)/shard_map/ppermute | solution.py:35
  71.3 5.1 %collective-permute-done.20.two_ref = bf16[256,1024]{1,0:T(8,128)(2,1)S(1)} collective-permute-done((bf16[256,1024]{1,0:T(8,128)(2,1)S(1)}, bf16[256,1024]{1,0:T(8,128)(2,1)S(1)}, u32[]{:S(2)}, u32[]{:S(2)}) %collective-permute-start.20) | collective-permute-done | bytes 524320 | tf_op jit(solution)/shard_map/ppermute | solution.py:35
  77.6 1.9 %collective-permute-start.21 = (bf16[64,2944]{1,0:T(8,128)(2,1)S(1)}, bf16[64,2944]{1,0:T(8,128)(2,1)S(1)}, u32[]{:S(2)}, u32[]{:S(2)}) collective-permute-start(bf16[64,2944]{1,0:T(8,128)(2,1)S(1)} %shard_map.74), channel_id=1, source_target_pairs={{0,8},{8,0},{16,24},{24,16},{1,9},{9,1},{17,25},{25,17},{2,10},{10... | collective-permute-start | bytes 1130504 | tf_op jit(solution)/shard_map/ppermute | solution.py:35
  79.6 13.5 %collective-permute-done.15 = bf16[64,1024]{1,0:T(8,128)(2,1)S(1)} collective-permute-done((bf16[64,1024]{1,0:T(8,128)(2,1)S(1)}, bf16[64,1024]{1,0:T(8,128)(2,1)S(1)}, u32[]{:S(2)}, u32[]{:S(2)}) %collective-permute-start.15) | collective-permute-done | bytes 131104 | tf_op jit(solution)/shard_map/ppermute | solution.py:55
  93.1 3.0 %collective-permute-start.16 = (bf16[64,1024]{1,0:T(8,128)(2,1)S(1)}, bf16[64,1024]{1,0:T(8,128)(2,1)S(1)}, u32[]{:S(2)}, u32[]{:S(2)}) collective-permute-start(bf16[64,1024]{1,0:T(8,128)(2,1)S(1)} %add_add_fusion.after_ref.t0), channel_id=1, source_target_pairs={{0,24},{8,0},{16,8},{24,16},{1,25},{9,1},{17,9},{25,17},{2,26},{10... | collective-permute-start | bytes 393224 | tf_op jit(solution)/shard_map/ppermute | solution.py:39
  96.2 3.4 %collective-permute-start.17 = (bf16[64,1024]{1,0:T(8,128)(2,1)S(1)}, bf16[64,1024]{1,0:T(8,128)(2,1)S(1)}, u32[]{:S(2)}, u32[]{:S(2)}) collective-permute-start(bf16[64,1024]{1,0:T(8,128)(2,1)S(1)} %add_add_fusion.after_ref.t0), channel_id=1, source_target_pairs={{0,16},{8,24},{16,0},{24,8},{1,17},{9,25},{17,1},{25,9},{2,18},{10... | collective-permute-start | bytes 393224 | tf_op jit(solution)/shard_map/ppermute | solution.py:39
  102.7 3.0 %collective-permute-done.17.t2 = bf16[64,1024]{1,0:T(8,128)(2,1)S(1)} collective-permute-done((bf16[64,1024]{1,0:T(8,128)(2,1)S(1)}, bf16[64,1024]{1,0:T(8,128)(2,1)S(1)}, u32[]{:S(2)}, u32[]{:S(2)}) %collective-permute-start.17) | collective-permute-done | bytes 131104 | tf_op jit(solution)/shard_map/ppermute | solution.py:39
  105.7 2.0 %collective-permute-done.18.t3 = bf16[64,1024]{1,0:T(8,128)(2,1)S(1)} collective-permute-done((bf16[64,1024]{1,0:T(8,128)(2,1)S(1)}, bf16[64,1024]{1,0:T(8,128)(2,1)S(1)}, u32[]{:S(2)}, u32[]{:S(2)}) %collective-permute-start.18) | collective-permute-done | bytes 131104 | tf_op jit(solution)/shard_map/ppermute | solution.py:39
  107.7 3.7 %shard_map.75 = bf16[64,2560]{1,0:T(8,128)(2,1)} custom-call(s32[4]{0:T(128)S(1)} %pad_add_fusion.where_ref, bf16[64,2560]{1,0:T(8,128)(2,1)S(1)} %bitcast.15, bf16[64,1024]{1,0:T(8,128)(2,1)S(1)} %add_add_fusion.after_ref.t0, bf16[64,1024]{1,0:T(8,128)(2,1)S(1)} %collective-permute-done.16.t1, bf16[64,1024]{1,0:T(8,128)(2,1)S(1)} %collective-permute-done.17.t2, ...), custom_call_target="tpu_custom_call" | custom-call | flops 83886080 | bytes 3000000 | tf_op jit(solution)/shard_map/pallas_call | solution.py:358
  (53 shorter events, 18.5 us)
Async XLA Ops:
  0.0 9.9 %collective-permute-start.1 = (bf16[16,1024]{1,0:T(8,128)(2,1)}, bf16[16,1024]{1,0:T(8,128)(2,1)S(1)}, u32[]{:S(2)}, u32[]{:S(2)}) collective-permute-start(bf16[16,1024]{1,0:T(8,128)(2,1)} %bitcast.16), channel_id=1, source_target_pairs={{0,256},{2,258},{4,260},{6,262},{256,0},{258,2},{260,4},{262,6},{1... | collective-permute-start | bytes 98312 | tf_op jit(solution)/shard_map/ppermute | solution.py:43
  11.0 11.8 %copy-start.5 = (bf16[1,16,1024]{2,1,0:T(8,128)(2,1)S(1)}, bf16[1,16,1024]{2,1,0:T(8,128)(2,1)}, u32[]{:S(2)}) copy-start(bf16[1,16,1024]{2,1,0:T(8,128)(2,1)} %param.10) | copy-start | bytes 98308
  12.6 28.5 %collective-permute-start.2 = (bf16[3840,128]{1,0:T(8,128)(2,1)S(1)}, bf16[3840,128]{1,0:T(8,128)(2,1)S(1)}, u32[]{:S(2)}, u32[]{:S(2)}) collective-permute-start(bf16[3840,128]{1,0:T(8,128)(2,1)S(1)} %get-tuple-element.13), channel_id=1, source_target_pairs={{0,2},{2,0},{4,6},{6,4},{256,258},{258,256},{260,262},{262,260},{1... | collective-permute-start | bytes 2949128 | tf_op jit(solution)/shard_map/ppermute | solution.py:43
  15.5 25.6 %collective-permute-start.3 = (bf16[3840,128]{1,0:T(8,128)(2,1)S(1)}, bf16[3840,128]{1,0:T(8,128)(2,1)S(1)}, u32[]{:S(2)}, u32[]{:S(2)}) collective-permute-start(bf16[3840,128]{1,0:T(8,128)(2,1)S(1)} %get-tuple-element.14), channel_id=1, source_target_pairs={{0,262},{2,4},{4,2},{6,256},{256,6},{258,260},{260,258},{262,0},{1... | collective-permute-start | bytes 2949128 | tf_op jit(solution)/shard_map/ppermute | solution.py:43
  19.4 21.7 %collective-permute-start.6 = (bf16[64,2560]{1,0:T(8,128)(2,1)S(1)}, bf16[64,2560]{1,0:T(8,128)(2,1)S(1)}, u32[]{:S(2)}, u32[]{:S(2)}) collective-permute-start(bf16[64,2560]{1,0:T(8,128)(2,1)S(1)} %bitcast.13), channel_id=1, source_target_pairs={{0,8},{8,0},{16,24},{24,16},{1,9},{9,1},{17,25},{25,17},{2,10},{10... | collective-permute-start | bytes 983048 | tf_op jit(solution)/shard_map/ppermute | solution.py:35
  22.8 10.1 %collective-permute-start.4 = (bf16[32,1024]{1,0:T(8,128)(2,1)S(1)}, bf16[32,1024]{1,0:T(8,128)(2,1)S(1)}, u32[]{:S(2)}, u32[]{:S(2)}) collective-permute-start(bf16[32,1024]{1,0:T(8,128)(2,1)S(1)} %shard_map.65.refs_0_), channel_id=1, source_target_pairs={{0,128},{32,160},{64,192},{96,224},{128,0},{160,32},{192,64},{224,... | collective-permute-start | bytes 196616 | tf_op jit(solution)/shard_map/ppermute | solution.py:47
  32.9 8.2 %collective-permute-start.5 = (bf16[64,1024]{1,0:T(8,128)(2,1)S(1)}, bf16[64,1024]{1,0:T(8,128)(2,1)S(1)}, u32[]{:S(2)}, u32[]{:S(2)}) collective-permute-start(bf16[64,1024]{1,0:T(8,128)(2,1)S(1)} %shard_map.66.refs_0_), channel_id=1, source_target_pairs={{0,64},{32,96},{64,0},{96,32},{128,192},{160,224},{192,128},{224,1... | collective-permute-start | bytes 393224 | tf_op jit(solution)/shard_map/ppermute | solution.py:47
  37.2 11.9 %collective-permute-start = (bf16[5120,128]{1,0:T(8,128)(2,1)}, bf16[5120,128]{1,0:T(8,128)(2,1)}, u32[]{:S(2)}, u32[]{:S(2)}) collective-permute-start(bf16[5120,128]{1,0:T(8,128)(2,1)} %own.1), channel_id=1, source_target_pairs={{0,1},{1,0},{2,3},{3,2},{4,5},{5,4},{6,7},{7,6},{8,9},{9,8},{10,11... | collective-permute-start | bytes 3932168 | tf_op jit(solution)/shard_map/ppermute | solution.py:51
  42.3 6.8 %collective-permute-start.7 = (bf16[5120,128]{1,0:T(8,128)(2,1)}, bf16[5120,128]{1,0:T(8,128)(2,1)}, u32[]{:S(2)}, u32[]{:S(2)}) collective-permute-start(bf16[5120,128]{1,0:T(8,128)(2,1)} %shard_map.68), channel_id=1, source_target_pairs={{0,1},{1,0},{2,3},{3,2},{4,5},{5,4},{6,7},{7,6},{8,9},{9,8},{10,11... | collective-permute-start | bytes 3932168 | tf_op jit(solution)/shard_map/ppermute | solution.py:51
  44.9 12.0 %collective-permute-start.19 = (bf16[128,1024]{1,0:T(8,128)(2,1)S(1)}, bf16[128,1024]{1,0:T(8,128)(2,1)S(1)}, u32[]{:S(2)}, u32[]{:S(2)}) collective-permute-start(bf16[128,1024]{1,0:T(8,128)(2,1)S(1)} %shard_map.67.piece_ref.refs_0_), channel_id=1, source_target_pairs={{0,32},{32,0},{64,96},{96,64},{128,160},{160,128},{192,224},{224,1... | collective-permute-start | bytes 786440 | tf_op jit(solution)/shard_map/ppermute | solution.py:47
  52.1 12.6 %copy-start.6 = (f32[512]{0:T(512)S(1)}, f32[512]{0:T(512)}, u32[]{:S(2)}) copy-start(f32[512]{0:T(512)} %param.8) | copy-start | bytes 6148
  52.2 6.3 %collective-permute-start.8 = (bf16[64,512]{1,0:T(8,128)(2,1)S(1)}, bf16[64,512]{1,0:T(8,128)(2,1)S(1)}, u32[]{:S(2)}, u32[]{:S(2)}) collective-permute-start(bf16[64,512]{1,0:T(8,128)(2,1)S(1)} %get-tuple-element.16), channel_id=1, source_target_pairs={{0,2},{2,0},{4,6},{6,4},{256,258},{258,256},{260,262},{262,260},{1... | collective-permute-start | bytes 196616 | tf_op jit(solution)/shard_map/ppermute | solution.py:43
  54.2 6.2 %collective-permute-start.9 = (bf16[64,512]{1,0:T(8,128)(2,1)S(1)}, bf16[64,512]{1,0:T(8,128)(2,1)S(1)}, u32[]{:S(2)}, u32[]{:S(2)}) collective-permute-start(bf16[64,512]{1,0:T(8,128)(2,1)S(1)} %get-tuple-element.17), channel_id=1, source_target_pairs={{0,262},{2,4},{4,2},{6,256},{256,6},{258,260},{260,258},{262,0},{1... | collective-permute-start | bytes 196616 | tf_op jit(solution)/shard_map/ppermute | solution.py:43
  60.4 16.0 %collective-permute-start.20 = (bf16[256,1024]{1,0:T(8,128)(2,1)S(1)}, bf16[256,1024]{1,0:T(8,128)(2,1)S(1)}, u32[]{:S(2)}, u32[]{:S(2)}) collective-permute-start(bf16[256,1024]{1,0:T(8,128)(2,1)S(1)} %shard_map.72.one_ref), channel_id=1, source_target_pairs={{0,24},{8,16},{16,8},{24,0},{1,25},{9,17},{17,9},{25,1},{2,26},{10... | collective-permute-start | bytes 1572872 | tf_op jit(solution)/shard_map/ppermute | solution.py:35
  66.5 2.1 %collective-permute-start.10 = (bf16[64,1024]{1,0:T(8,128)(2,1)S(1)}, bf16[64,1024]{1,0:T(8,128)(2,1)S(1)}, u32[]{:S(2)}, u32[]{:S(2)}) collective-permute-start(bf16[64,1024]{1,0:T(8,128)(2,1)S(1)} %shard_map.70.own_ref), channel_id=1, source_target_pairs={{0,256},{1,257},{2,258},{3,259},{4,260},{5,261},{6,262},{7,263},{8... | collective-permute-start | bytes 393224 | tf_op jit(solution)/shard_map/ppermute | solution.py:55
  67.2 1.4 %collective-permute-start.11 = (bf16[64,1024]{1,0:T(8,128)(2,1)S(1)}, bf16[64,1024]{1,0:T(8,128)(2,1)S(1)}, u32[]{:S(2)}, u32[]{:S(2)}) collective-permute-start(bf16[64,1024]{1,0:T(8,128)(2,1)S(1)} %shard_map.70.own_ref), channel_id=1, source_target_pairs={{0,64},{1,65},{2,66},{3,67},{4,68},{5,69},{6,70},{7,71},{8,72},{9,... | collective-permute-start | bytes 393224 | tf_op jit(solution)/shard_map/ppermute | solution.py:55
  67.8 0.7 collective-permute-start.12
  68.7 10.9 %collective-permute-start.13 = (bf16[64,1024]{1,0:T(8,128)(2,1)S(1)}, bf16[64,1024]{1,0:T(8,128)(2,1)S(1)}, u32[]{:S(2)}, u32[]{:S(2)}) collective-permute-start(bf16[64,1024]{1,0:T(8,128)(2,1)S(1)} %shard_map.71.after_ref), channel_id=1, source_target_pairs={{0,128},{64,320},{192,448},{256,384},{1,129},{65,321},{193,449},{2... | collective-permute-start | bytes 393224 | tf_op jit(solution)/shard_map/ppermute | solution.py:55
  69.3 10.2 %collective-permute-start.14 = (bf16[64,1024]{1,0:T(8,128)(2,1)S(1)}, bf16[64,1024]{1,0:T(8,128)(2,1)S(1)}, u32[]{:S(2)}, u32[]{:S(2)}) collective-permute-start(bf16[64,1024]{1,0:T(8,128)(2,1)S(1)} %shard_map.71.after_ref), channel_id=1, source_target_pairs={{0,32},{64,96},{192,160},{256,288},{1,33},{65,97},{193,161},{257,2... | collective-permute-start | bytes 393224 | tf_op jit(solution)/shard_map/ppermute | solution.py:55
  70.0 23.1 %collective-permute-start.15 = (bf16[64,1024]{1,0:T(8,128)(2,1)S(1)}, bf16[64,1024]{1,0:T(8,128)(2,1)S(1)}, u32[]{:S(2)}, u32[]{:S(2)}) collective-permute-start(bf16[64,1024]{1,0:T(8,128)(2,1)S(1)} %shard_map.71.after_ref), channel_id=1, source_target_pairs={{0,224},{64,352},{192,416},{256,480},{1,225},{65,353},{193,417},{2... | collective-permute-start | bytes 393224 | tf_op jit(solution)/shard_map/ppermute | solution.py:55
  77.6 30.1 %collective-permute-start.21 = (bf16[64,2944]{1,0:T(8,128)(2,1)S(1)}, bf16[64,2944]{1,0:T(8,128)(2,1)S(1)}, u32[]{:S(2)}, u32[]{:S(2)}) collective-permute-start(bf16[64,2944]{1,0:T(8,128)(2,1)S(1)} %shard_map.74), channel_id=1, source_target_pairs={{0,8},{8,0},{16,24},{24,16},{1,9},{9,1},{17,25},{25,17},{2,10},{10... | collective-permute-start | bytes 1130504 | tf_op jit(solution)/shard_map/ppermute | solution.py:35
  93.1 9.6 %collective-permute-start.16 = (bf16[64,1024]{1,0:T(8,128)(2,1)S(1)}, bf16[64,1024]{1,0:T(8,128)(2,1)S(1)}, u32[]{:S(2)}, u32[]{:S(2)}) collective-permute-start(bf16[64,1024]{1,0:T(8,128)(2,1)S(1)} %add_add_fusion.after_ref.t0), channel_id=1, source_target_pairs={{0,24},{8,0},{16,8},{24,16},{1,25},{9,1},{17,9},{25,17},{2,26},{10... | collective-permute-start | bytes 393224 | tf_op jit(solution)/shard_map/ppermute | solution.py:39
  96.2 9.5 %collective-permute-start.17 = (bf16[64,1024]{1,0:T(8,128)(2,1)S(1)}, bf16[64,1024]{1,0:T(8,128)(2,1)S(1)}, u32[]{:S(2)}, u32[]{:S(2)}) collective-permute-start(bf16[64,1024]{1,0:T(8,128)(2,1)S(1)} %add_add_fusion.after_ref.t0), channel_id=1, source_target_pairs={{0,16},{8,24},{16,0},{24,8},{1,17},{9,25},{17,1},{25,9},{2,18},{10... | collective-permute-start | bytes 393224 | tf_op jit(solution)/shard_map/ppermute | solution.py:39
  99.6 8.1 %collective-permute-start.18 = (bf16[64,1024]{1,0:T(8,128)(2,1)S(1)}, bf16[64,1024]{1,0:T(8,128)(2,1)S(1)}, u32[]{:S(2)}, u32[]{:S(2)}) collective-permute-start(bf16[64,1024]{1,0:T(8,128)(2,1)S(1)} %add_add_fusion.after_ref.t0), channel_id=1, source_target_pairs={{0,8},{8,16},{16,24},{24,0},{1,9},{9,17},{17,25},{25,1},{2,10},{10... | collective-permute-start | bytes 393224 | tf_op jit(solution)/shard_map/ppermute | solution.py:39
  (5 other events, 26.7 us)
